TPU v7x, 32 devices: a whole 2x2x4 slice. The times are simulated.
32 devices in a mesh: row: 4 (over z), col: 8 (over y, x, core).
Axes of the slice: x: 2, y: 2, z: 4, core: 2. Of those that a mesh axis runs over, the one named last changes fastest.
Arguments:
- x_vec: float32 [4, 524288], P(None, ('col', 'row'))
- hx_vec: float32 [4, 524288], P(None, ('col', 'row'))
- p_vec: float32 [4, 524288], P(None, ('col', 'row'))
- hp_vec: float32 [4, 524288], P(None, ('col', 'row'))
- theta: float32 [4], replicated, may hold values from 0.5 to 2
- precond: float32 [524288], P(('col', 'row')), may hold values from 1 to 4
- tile_vals: bfloat16 [4, 8, 1024, 4096], P('row', 'col'), may hold values from -0.25 to 0.25
- tile_rows: int32 [4, 8, 1024], P('row', 'col'), may hold values from 0 to 1023
- tile_cols: int32 [4, 8, 1024], P('row', 'col'), may hold values from 0 to 1023
- tile_count: int32 [4, 8], P('row', 'col'), may hold values from 128 to 1024, as said below
Outputs:
- hw_vec: float32 [4, 524288], P(None, ('col', 'row'))
- gram_a: float32 [12, 12], replicated
- gram_b: float32 [12, 12], replicated
Inputs may be any that keep to these rules, and one draw needn't show every extreme that they name: `tile_count`: some tile uses all 1024 slots and some tile uses 1024 // 8.
All inputs are finite; a program needn't handle non-finite values.
Results may differ from a plain program's by a relative error of at most 0.0029.
Values may be sent and summed in bfloat16 or wider, within the bound.
A program may use at most 192 MiB of HBM per device.

v0:
```python
import jax
import jax.numpy as jnp
from jax import lax
from jax.sharding import PartitionSpec as P

BLOCK = 64


def from_behind(block, axis, distance):
    devices = range(lax.axis_size(axis))
    route = [((i - distance) % len(devices), i) for i in devices]
    return lax.ppermute(block, axis, route)


def segment_blocks(part, index, block_total):
    summed = jax.ops.segment_sum(part, index, num_segments=block_total)
    return jnp.transpose(summed, (1, 0, 2)).reshape(part.shape[1], -1)


def tile_terms(values, row_index, col_index, live_mask, col_vec, row_vec):
    vec_count = col_vec.shape[0]
    block_size = values.shape[1]
    blocks_col = col_vec.reshape(vec_count, -1, block_size)
    blocks_row = row_vec.reshape(vec_count, -1, block_size)
    block_total = blocks_col.shape[1]
    picked_col = blocks_col[:, col_index, :]
    picked_row = blocks_row[:, row_index, :]
    forward_part = (
        jnp.einsum("zij,kzj->zki", values, picked_col, preferred_element_type=jnp.float32)
        * live_mask[:, None, None]
    )
    transpose_part = (
        jnp.einsum("zij,kzi->zkj", values, picked_row, preferred_element_type=jnp.float32)
        * live_mask[:, None, None]
    )
    return (
        segment_blocks(forward_part, row_index, block_total),
        segment_blocks(transpose_part, col_index, block_total),
    )


def body(x_vec, hx_vec, p_vec, hp_vec, theta, precond, tile_vals, tile_rows, tile_cols, tile_count):
    vec_count, piece_len = x_vec.shape
    row_count = lax.axis_size("row")
    col_count = lax.axis_size("col")
    bit_count = row_count.bit_length() - 1
    row_pos = lax.axis_index("row")
    ndim_total = piece_len * row_count * col_count
    residue = (hx_vec - x_vec * theta[:, None]) / precond[None, :]
    w_send = residue.astype(jnp.bfloat16)
    vectors = jnp.concatenate([x_vec, residue, p_vec], 0)
    local_b = jnp.dot(
        vectors, vectors.T, precision=lax.Precision.HIGHEST, preferred_element_type=jnp.float32
    )
    correlation_sum = lax.psum(local_b, ("row", "col"))
    slot_total = tile_vals.shape[2]
    values = tile_vals[0, 0].reshape(slot_total, BLOCK, BLOCK)
    row_index = tile_rows[0, 0]
    col_index = tile_cols[0, 0]
    live_mask = (jnp.arange(slot_total, dtype=jnp.int32) < tile_count[0, 0]).astype(jnp.float32)
    own_segment = lax.all_gather(w_send, "row", axis=1, tiled=True)
    carried = own_segment
    for bit_pos in range(bit_count):
        shifted = from_behind(carried, "col", -(1 << bit_pos))
        carried = jnp.where(row_pos >> bit_pos & 1 == 1, shifted, carried)
    far_segment = carried
    forward_seg, transpose_seg = tile_terms(
        values, row_index, col_index, live_mask, own_segment, far_segment
    )
    carried = forward_seg
    for bit_pos in range(bit_count):
        shifted = from_behind(carried, "col", 1 << bit_pos)
        carried = jnp.where(row_pos >> bit_pos & 1 == 1, shifted, carried)
    hw_vec = lax.psum_scatter(carried + transpose_seg, "row", scatter_dimension=1, tiled=True)
    images = jnp.concatenate([hx_vec, hw_vec, hp_vec], 0)
    local_a = jnp.dot(
        vectors, images.T, precision=lax.Precision.HIGHEST, preferred_element_type=jnp.float32
    )
    projected_sum = lax.psum(local_a, ("row", "col"))
    return (hw_vec, projected_sum / ndim_total, correlation_sum / ndim_total)


def solution(mesh):
    placed = (
        P(None, ("col", "row")),
        P(None, ("col", "row")),
        P(None, ("col", "row")),
        P(None, ("col", "row")),
        P(),
        P(("col", "row")),
        P("row", "col", None, None),
        P("row", "col", None),
        P("row", "col", None),
        P("row", "col"),
    )
    return jax.shard_map(
        body,
        mesh=mesh,
        in_specs=placed,
        out_specs=(P(None, ("col", "row")), P(), P()),
        check_vma=False,
    )
```

profile of v0, /device:TPU:0, one launch (start us, length us, event | category | flops | bytes accessed | tf_op | source)
XLA Modules:
  0.0 882.7 jit_solution(5856095951039342927)
XLA Ops:
  7.2 0.0 reduce-scatter.4.cloned.1.call-start
  7.2 1.2 fusion.12
  8.4 17.4 %all_gather.3 = bf16[4,65536]{1,0:T(4,128)(2,1)S(1)} all-gather(bf16[4,16384]{1,0:T(4,128)(2,1)S(1)} %get-tuple-element.5), channel_id=1, replica_groups=mesh['row'=4,'col'=8] {'row'}, dimensions={1}, use_global_device_ids=true | all-gather | bytes 655360 | tf_op jit(solution)/shard_map/all_gather | solution.py:61
  25.8 0.4 collective-permute-start.2
  26.2 0.8 reshape.81
  27.1 12.0 %copy.21 = bf16[1,1,1024,4096]{2,3,1,0:T(8,128)(2,1)} copy(bf16[1,1,1024,4096]{3,2,1,0:T(8,128)(2,1)} %param.16) | data formatting | bytes 16777216 | tf_op args[6]
  39.1 23.9 %copy.22 = bf16[1024,64,64]{2,1,0:T(8,128)(2,1)} copy(bf16[1024,64,64]{0,2,1:T(8,128)(2,1)} %bitcast.24) | data formatting | bytes 16777216 | tf_op jit(solution)/shard_map/reshape;squeeze | solution.py:57
  63.7 0.8 copy.20
  64.5 0.0 copy-done.4
  64.5 3.6 gather_fusion
  68.1 0.0 collective-permute-done.2
  68.1 0.3 broadcast_select_fusion
  68.4 2.1 collective-permute-start.3
  70.5 13.3 %convolution_multiply_fusion.1 = f32[1024,4,64]{2,1,0:T(4,128)} fusion(bf16[1024,64,64]{2,1,0:T(8,128)(2,1)} %copy.22, bf16[1024,4,64]{2,1,0:T(4,128)(2,1)S(1)} %gather_fusion, f32[1024]{0:T(1024)S(1)} %fusion.9), kind=kOutput, calls=%fused_computation.5 | convolution fusion | flops 33816576 | bytes 9965568 | tf_op jit(solution)/shard_map/zij,kzj->zki/dot_general | solution.py:29
  83.7 0.3 broadcast.48.clone.1
  84.0 0.4 copy-done.3
  84.4 66.3 %scatter_fusion = f32[1024,4,64]{2,1,0:T(4,128)S(1)} fusion(f32[1024,4,64]{2,1,0:T(4,128)S(1)} %broadcast.48.clone.1, s32[1024]{0:T(1024)S(1)} %bitcast.30, f32[1024,4,64]{2,1,0:T(4,128)} %convolution_multiply_fusion.1), kind=kCustom, calls=%fused_computation.2 | custom fusion | flops 262144 | bytes 3149824 | tf_op jit(solution)/shard_map/scatter-add | solution.py:16
  150.8 1.5 copy.23
  152.2 2.4 reshape.82
  154.7 0.3 collective-permute-start
  154.9 0.0 collective-permute-done.3
  155.0 0.3 broadcast_select_fusion.2
  155.2 0.8 reshape.83
  156.1 0.8 copy.24
  156.9 13.1 %collective-permute-done = f32[4,65536]{1,0:T(4,128)} collective-permute-done((f32[4,65536]{1,0:T(4,128)S(1)}, f32[4,65536]{1,0:T(4,128)}, u32[]{:S(2)}, u32[]{:S(2)}) %collective-permute-start) | collective-permute-done | bytes 1048608 | tf_op jit(solution)/shard_map/ppermute | solution.py:12
  169.9 0.3 broadcast_select_fusion.1
  170.2 0.2 collective-permute-start.1
  170.5 3.6 gather_fusion.1
  174.0 9.1 %convolution_multiply_fusion = f32[1024,4,64]{2,1,0:T(4,128)} fusion(bf16[1024,64,64]{2,1,0:T(8,128)(2,1)} %copy.22, bf16[1024,4,64]{2,1,0:T(4,128)(2,1)S(1)} %gather_fusion.1, f32[1024]{0:T(1024)S(1)} %fusion.9), kind=kOutput, calls=%fused_computation.4 | convolution fusion | flops 33816576 | bytes 9965568 | tf_op jit(solution)/shard_map/zij,kzi->zkj/dot_general | solution.py:33
  183.1 0.3 broadcast.48.clone
  183.4 66.3 %scatter_fusion.1 = f32[1024,4,64]{2,1,0:T(4,128)S(1)} fusion(f32[1024,4,64]{2,1,0:T(4,128)S(1)} %broadcast.48.clone, s32[1024]{0:T(1024)S(1)} %bitcast.31, f32[1024,4,64]{2,1,0:T(4,128)} %convolution_multiply_fusion), kind=kCustom, calls=%fused_computation.3 | custom fusion | flops 262144 | bytes 3149824 | tf_op jit(solution)/shard_map/scatter-add | solution.py:16
  249.7 1.5 copy.26
  251.2 2.4 reshape.84
  253.6 0.0 collective-permute-done.1
  253.6 0.4 select_add_fusion
  254.0 16.0 %copy.27 = f32[4,65536]{0,1:T(8,128)} copy(f32[4,65536]{1,0:T(4,128)S(1)} %select_add_fusion) | data formatting | bytes 2097152
  270.1 0.0 reduce-scatter.4.cloned.1.call-update
  270.1 0.9 copy-done.1
  271.0 0.1 copy-done.6
  271.1 1.4 fusion.8
  272.5 554.5 %reduce-scatter.4.cloned.1.call-done = f32[16384,4]{1,0:T(8,128)} async-done(((f32[65536,4]{1,0:T(8,128)}), f32[16384,4]{1,0:T(8,128)}) %reduce-scatter.4.cloned.1.call-update) | async-done | bytes 262160
  827.0 5.5 copy.28
  832.5 0.0 copy-done
  832.5 0.0 copy-start.2
  832.5 1.6 fusion
  834.1 41.1 %all-reduce = (f32[12,12]{1,0:T(8,128)S(1)}, f32[12,12]{1,0:T(8,128)S(1)}) all-reduce(f32[12,12]{1,0:T(8,128)S(1)} %fusion, f32[12,12]{1,0:T(8,128)S(1)} %fusion.8), channel_id=1, replica_groups=mesh['row'=4,'col'=8] {'row','col'}, use_global_device_ids=true, to_apply=%region_3.4 | all-reduce | flops 288 | bytes 2304 | tf_op jit(solution)/shard_map/psum | solution.py:79
  875.2 0.6 broadcast_multiply_fusion
  875.8 0.0 copy-done.2
  (12 shorter events, 0.0 us)
Async XLA Ops:
  7.2 819.8 %reduce-scatter.4.cloned.1.call-start = ((), (), s32[]{:S(2)}) async-start(), calls=%async_computation.1 | async-start | bytes 41943040
  25.8 42.3 %collective-permute-start.2 = (bf16[4,65536]{1,0:T(4,128)(2,1)S(1)}, bf16[4,65536]{1,0:T(4,128)(2,1)S(1)}, u32[]{:S(2)}, u32[]{:S(2)}) collective-permute-start(bf16[4,65536]{1,0:T(4,128)(2,1)S(1)} %all_gather.3), channel_id=1, source_target_pairs={{1,0},{2,1},{3,2},{4,3},{5,4},{6,5},{7,6},{0,7},{9,8},{10,9},{11,1... | collective-permute-start | bytes 1572872 | tf_op jit(solution)/shard_map/ppermute | solution.py:12
  63.0 1.5 copy-start.4
  68.4 86.5 %collective-permute-start.3 = (bf16[4,65536]{1,0:T(4,128)(2,1)S(1)}, bf16[4,65536]{1,0:T(4,128)(2,1)S(1)}, u32[]{:S(2)}, u32[]{:S(2)}) collective-permute-start(bf16[4,65536]{1,0:T(4,128)(2,1)S(1)} %broadcast_select_fusion), channel_id=1, source_target_pairs={{2,0},{3,1},{4,2},{5,3},{6,4},{7,5},{0,6},{1,7},{10,8},{11,9},{12,... | collective-permute-start | bytes 1572872 | tf_op jit(solution)/shard_map/ppermute | solution.py:12
  83.7 0.7 copy-start.3
  154.7 15.3 %collective-permute-start = (f32[4,65536]{1,0:T(4,128)S(1)}, f32[4,65536]{1,0:T(4,128)}, u32[]{:S(2)}, u32[]{:S(2)}) collective-permute-start(f32[4,65536]{1,0:T(4,128)S(1)} %reshape.82), channel_id=1, source_target_pairs={{7,0},{0,1},{1,2},{2,3},{3,4},{4,5},{5,6},{6,7},{15,8},{8,9},{9,10... | collective-permute-start | bytes 3145736 | tf_op jit(solution)/shard_map/ppermute | solution.py:12
  170.2 83.4 %collective-permute-start.1 = (f32[4,65536]{1,0:T(4,128)S(1)}, f32[4,65536]{1,0:T(4,128)}, u32[]{:S(2)}, u32[]{:S(2)}) collective-permute-start(f32[4,65536]{1,0:T(4,128)S(1)} %broadcast_select_fusion.1), channel_id=1, source_target_pairs={{6,0},{7,1},{0,2},{1,3},{2,4},{3,5},{4,6},{5,7},{14,8},{15,9},{8,1... | collective-permute-start | bytes 3145736 | tf_op jit(solution)/shard_map/ppermute | solution.py:12
  270.1 0.9 copy-start.1
  270.1 1.0 copy-start.6
  827.0 5.5 copy-start
  827.0 5.5 copy-start.5
  832.5 43.3 %copy-start.2 = (f32[4,16384]{1,0:T(4,128)}, f32[4,16384]{1,0:T(4,128)S(1)}, u32[]{:S(2)}) copy-start(f32[4,16384]{1,0:T(4,128)S(1)} %copy.28) | copy-start | bytes 786436
Sparse Core Ops, SparseCore 0:
  270.2 556.7 reduce-scatter.3
where the time goes:
time: 893 us; the launch traced here: 883 us
  waiting for transfers between devices  568 us (64%)
  other arithmetic  136 us (15%)
  local copies, waits for them, and re-layouts  77.7 us (9%)
  blocking collectives  58.5 us (7%)
  matrix products  25.4 us (3%)
  between operations  14.9 us (2%)
    unnamed x2, waiting for transfers between devices  554 us
    scatter-add x2, other arithmetic, segment_blocks(): summed = jax.ops.segment_sum(part, index, num_segments=block_total)  133 us
    psum x1, blocking collectives, body(): projected_sum = lax.psum(local_a, ('row', 'col'))  41.1 us
    unnamed x17, local copies, waits for them, and re-layouts  35 us
    another operation x1, local copies, waits for them, and re-layouts, body(): values = tile_vals[0, 0].reshape(slot_total, BLOCK, BLOCK)  23.9 us
  transfers between devices with their start and end apart: 5, of which 2 were waited for; matrix products, arithmetic and copies ran while one was open for 24% of the time, Pallas kernels for 0%

commit v1 on v0

v1 whole, which is shorter than its diff:
```python
import functools
import jax
import jax.numpy as jnp
from jax import lax
from jax.experimental import pallas as pl
from jax.experimental.pallas import tpu as pltpu
from jax.sharding import PartitionSpec as P

BLOCK = 64
GROUPS = 4
MESH = pl.DeviceIdType.MESH
F32 = jnp.float32
BF16 = jnp.bfloat16
VMEM_BYTES = 58 * 1024 * 1024


def row_iota():
    return lax.broadcasted_iota(jnp.int32, (8, 128), 0)


def lane_iota():
    return lax.broadcasted_iota(jnp.int32, (8, 128), 1)


def spread_matrix():
    a = lax.broadcasted_iota(jnp.int32, (128, 128), 0)
    b = lax.broadcasted_iota(jnp.int32, (128, 128), 1)
    return jnp.where((a % 64) == 2 * (b % 32) + a // 64, 1.0, 0.0).astype(BF16)


def gather_kernel(w_ref, own_ref, far_ref, up_send, up_recv, down_send, down_recv, far_send, far_recv):
    n = own_ref.shape[0]
    cols = lax.axis_size("col")
    r, c = lax.axis_index("row"), lax.axis_index("col")
    source = lax.rem(c + r, cols)
    target = lax.rem(c - r + cols, cols)
    barrier = pltpu.get_barrier_semaphore()

    def greet(row, col):
        pl.semaphore_signal(barrier, inc=1, device_id=(row, col), device_id_type=MESH)

    pl.when(r > 0)(lambda: greet(r - 1, c))
    pl.when(r < n - 1)(lambda: greet(r + 1, c))
    pl.when(r > 0)(lambda: greet(r, source))
    own_ref[r] = w_ref[...]
    pl.semaphore_wait(barrier, jnp.where(r > 0, jnp.where(r < n - 1, 3, 2), 1))

    def up_copy(piece, d):
        return pltpu.make_async_remote_copy(
            src_ref=own_ref.at[piece], dst_ref=own_ref.at[piece],
            send_sem=up_send.at[d], recv_sem=up_recv.at[d],
            device_id=(r + 1, c), device_id_type=MESH)

    def down_copy(piece, d):
        return pltpu.make_async_remote_copy(
            src_ref=own_ref.at[piece], dst_ref=own_ref.at[piece],
            send_sem=down_send.at[d], recv_sem=down_recv.at[d],
            device_id=(r - 1, c), device_id_type=MESH)

    def far_copy(piece, slot):
        return pltpu.make_async_remote_copy(
            src_ref=own_ref.at[piece], dst_ref=far_ref.at[piece],
            send_sem=far_send.at[slot], recv_sem=far_recv.at[slot],
            device_id=(r, target), device_id_type=MESH)

    pl.when(r < n - 1)(lambda: up_copy(r, 0).start())
    pl.when(r > 0)(lambda: down_copy(r, 0).start())
    pl.when(r > 0)(lambda: far_copy(r, 0).start())
    for d in range(1, n):
        @pl.when(r >= d)
        def _():
            up_copy(r - d, d - 1).wait_recv()
            pl.when(r < n - 1)(lambda: up_copy(r - d, d).start())
            far_copy(r - d, 2 * d - 1).start()

        @pl.when(r + d < n)
        def _():
            down_copy(r + d, d - 1).wait_recv()

            @pl.when(r > 0)
            def _():
                down_copy(r + d, d).start()
                far_copy(r + d, 2 * d).start()

    @pl.when(r == 0)
    def _():
        far_ref[...] = own_ref[...]

    for d in range(n):
        if d:
            @pl.when(r >= d)
            def _():
                far_copy(r - d, 2 * d - 1).wait()

            @pl.when((r + d < n) & (r > 0))
            def _():
                far_copy(r + d, 2 * d).wait()

            pl.when((r >= d) & (r < n - 1))(lambda: up_copy(r - d, d).wait_send())
            pl.when((r + d < n) & (r > 0))(lambda: down_copy(r + d, d).wait_send())
        else:
            pl.when(r > 0)(lambda: far_copy(r, 0).wait())
            pl.when(r < n - 1)(lambda: up_copy(r, 0).wait_send())
            pl.when(r > 0)(lambda: down_copy(r, 0).wait_send())


def gather_pieces(piece, n):
    shape = jax.ShapeDtypeStruct((n,) + piece.shape, piece.dtype)
    vmem = pl.BlockSpec(memory_space=pltpu.VMEM)
    dma = pltpu.SemaphoreType.DMA
    return pl.pallas_call(
        gather_kernel,
        out_shape=(shape, shape),
        in_specs=[vmem],
        out_specs=(vmem, vmem),
        scratch_shapes=[dma((n,)), dma((n,)), dma((n,)), dma((n,)), dma((2 * n,)), dma((2 * n,))],
        compiler_params=pltpu.CompilerParams(
            collective_id=0, has_side_effects=True, vmem_limit_bytes=VMEM_BYTES),
    )(piece)


def product_kernel(chunk, rows_ref, cols_ref, count_ref, vals_ref, own_ref, far_ref, fwd_ref, tr_ref,
                   x_col, x_row, acc_f, acc_t):
    step, steps = pl.program_id(0), pl.num_programs(0)
    n, _, width = own_ref.shape
    tiles = width // 128
    per_group = 2 * tiles
    nblk = n * GROUPS * per_group
    low = row_iota() < 4
    left = lane_iota() < 64
    keep = low == left
    quarter = lane_iota() // 32

    def block_at(q, g, t, parity):
        return q * (GROUPS * per_group) + g * per_group + 2 * t + parity

    def expand(src_ref, dst_ref):
        def tile(i, _):
            q, t = i // tiles, i % tiles
            s = src_ref[q, :, pl.ds(pl.multiple_of(t * 128, 128), 128)].astype(F32)
            for h in range(2):
                v = s[8 * h:8 * h + 8]
                vl = pltpu.roll(v, 64, 1)
                vs = pltpu.roll(v, 4, 0)
                vls = pltpu.roll(vl, 4, 0)
                dst_ref[block_at(q, 2 * h, t, 0)] = jnp.where(keep, jnp.where(low, v, vls), 0.0)
                dst_ref[block_at(q, 2 * h, t, 1)] = jnp.where(keep, jnp.where(low, vl, vs), 0.0)
                dst_ref[block_at(q, 2 * h + 1, t, 0)] = jnp.where(keep, jnp.where(low, vs, vl), 0.0)
                dst_ref[block_at(q, 2 * h + 1, t, 1)] = jnp.where(keep, jnp.where(low, vls, v), 0.0)
            return 0
        lax.fori_loop(0, n * tiles, tile, 0, unroll=4)

    @pl.when(step == 0)
    def _():
        expand(own_ref, x_col)
        expand(far_ref, x_row)
        spread = spread_matrix()

        def part(i, _):
            at = pl.ds(i * 32, 32)
            x = x_row[at].reshape(256, 128).astype(BF16)
            x_row[at] = jnp.dot(x, spread, preferred_element_type=F32).reshape(32, 8, 128)
            zero = jnp.zeros((32, 8, 128), F32)
            acc_f[at] = zero
            acc_t[at] = zero
            return 0
        lax.fori_loop(0, nblk // 32, part, 0)

    count = count_ref[0]
    first = step * chunk
    live = jnp.clip(count - first, 0, chunk)

    def octet(i, _):
        for half in range(2):
            at = i * 8 + half * 4
            w = vals_ref[pl.ds(pl.multiple_of(at * 32, 128), 128), :]
            rows, cols, lf, lt = [], [], [], []
            for z in range(4):
                slot = first + at + z
                r, c = rows_ref[slot], cols_ref[slot]
                lf.append(x_col[c])
                lt.append(jnp.where(quarter == z, x_row[r], 0.0))
                used = slot < count
                rows.append(jnp.where(used, r, nblk))
                cols.append(jnp.where(used, c, nblk))
            of = lax.dot_general(jnp.concatenate(lf, 0).astype(BF16), w, (((1,), (1,)), ((), ())),
                                 preferred_element_type=F32)
            ot = jnp.dot(jnp.concatenate(lt, 0).astype(BF16), w, preferred_element_type=F32)
            for z in range(4):
                acc_f[rows[z]] += jnp.where(quarter == z, of[8 * z:8 * z + 8], 0.0)
                acc_t[cols[z]] += ot[8 * z:8 * z + 8]
        return 0
    lax.fori_loop(0, (live + 7) // 8, octet, 0)

    @pl.when(step == steps - 1)
    def _():
        spread = spread_matrix()

        def part(i, _):
            at = pl.ds(i * 32, 32)
            x = acc_f[at].reshape(256, 128)
            hi = x.astype(BF16)
            lo = (x - hi.astype(F32)).astype(BF16)
            back = (((1,), (1,)), ((), ()))
            y = lax.dot_general(hi, spread, back, preferred_element_type=F32)
            y += lax.dot_general(lo, spread, back, preferred_element_type=F32)
            acc_f[at] = y.reshape(32, 8, 128)
            return 0
        lax.fori_loop(0, nblk // 32, part, 0)

        def fold(src_ref, dst_ref):
            def folded(q, g, t, parity):
                x = jnp.where(keep, src_ref[block_at(q, g, t, parity)], 0.0)
                return x + pltpu.roll(pltpu.roll(x, 64, 1), 4, 0)

            def tile(i, _):
                q, t = i // tiles, i % tiles
                out = []
                for h in range(2):
                    e0, o0 = folded(q, 2 * h, t, 0), folded(q, 2 * h, t, 1)
                    e1, o1 = folded(q, 2 * h + 1, t, 0), folded(q, 2 * h + 1, t, 1)
                    top = jnp.where(left, e0, pltpu.roll(o0, 4, 0))
                    bottom = jnp.where(left, pltpu.roll(e1, 4, 0), o1)
                    out.append(jnp.where(low, top, bottom))
                at = pl.ds(pl.multiple_of(t * 128, 128), 128)
                dst_ref[q, :, at] = jnp.concatenate(out, 0).astype(dst_ref.dtype)
                return 0
            lax.fori_loop(0, n * tiles, tile, 0, unroll=4)

        fold(acc_f, fwd_ref)
        fold(acc_t, tr_ref)


def block_products(vals, rows, cols, count, own, far):
    slots = rows.shape[0]
    chunk = 64
    n, depth, width = own.shape
    nblk = n * GROUPS * (width // 64)
    whole = pl.BlockSpec((n, depth, width), lambda i, *_: (0, 0, 0))
    return pl.pallas_call(
        functools.partial(product_kernel, chunk),
        out_shape=(jax.ShapeDtypeStruct(own.shape, BF16), jax.ShapeDtypeStruct(own.shape, F32)),
        grid_spec=pltpu.PrefetchScalarGridSpec(
            num_scalar_prefetch=3,
            grid=(slots // chunk,),
            in_specs=[pl.BlockSpec((chunk * 32, 128), lambda i, *_: (i, 0)), whole, whole],
            out_specs=(whole, whole),
            scratch_shapes=[
                pltpu.VMEM((nblk, 8, 128), F32),
                pltpu.VMEM((nblk, 8, 128), F32),
                pltpu.VMEM((nblk + 1, 8, 128), F32),
                pltpu.VMEM((nblk + 1, 8, 128), F32),
            ],
        ),
        compiler_params=pltpu.CompilerParams(vmem_limit_bytes=VMEM_BYTES),
    )(rows, cols, count, vals, own, far)


def reduce_kernel(fwd_ref, tr_ref, out_ref, far, stage, landed, far_send, far_recv, send, recv):
    n = fwd_ref.shape[0]
    cols = lax.axis_size("col")
    r, c = lax.axis_index("row"), lax.axis_index("col")
    target = lax.rem(c + r, cols)
    source = lax.rem(c - r + cols, cols)
    barrier = pltpu.get_barrier_semaphore()
    for d in range(1, n):
        pl.semaphore_signal(barrier, inc=1, device_id=(lax.rem(r + d, n), c), device_id_type=MESH)

    @pl.when(r > 0)
    def _():
        pl.semaphore_signal(barrier, inc=1, device_id=(r, source), device_id_type=MESH)
    pl.semaphore_wait(barrier, jnp.where(r > 0, n, n - 1))

    def far_copy(d):
        q = lax.rem(r + d, n)
        return pltpu.make_async_remote_copy(
            src_ref=fwd_ref.at[q], dst_ref=far.at[q],
            send_sem=far_send.at[d], recv_sem=far_recv.at[d],
            device_id=(r, target), device_id_type=MESH)

    def row_copy(d):
        return pltpu.make_async_remote_copy(
            src_ref=stage.at[d - 1], dst_ref=landed.at[d - 1],
            send_sem=send.at[d - 1], recv_sem=recv.at[d - 1],
            device_id=(lax.rem(r + d, n), c), device_id_type=MESH)

    order = list(range(1, n)) + [0]

    @pl.when(r > 0)
    def _():
        for d in order:
            far_copy(d).start()

    @pl.when(r == 0)
    def _():
        far[...] = fwd_ref[...]

    for d in order:
        pl.when(r > 0)(lambda: far_copy(d).wait_recv())
        q = lax.rem(r + d, n)
        total = tr_ref[q] + far[q].astype(F32)
        if d:
            stage[d - 1] = total.astype(BF16)
            row_copy(d).start()
    for d in range(1, n):
        row_copy(d).wait_recv()
        total += landed[d - 1].astype(F32)
    width = total.shape[1]
    for g in range(GROUPS):
        out_ref[:, g * width:(g + 1) * width] = total[4 * g:4 * g + 4]
    for d in range(1, n):
        row_copy(d).wait_send()

    @pl.when(r > 0)
    def _():
        for d in order:
            far_copy(d).wait_send()


def reduce_pieces(fwd, tr):
    n, depth, width = fwd.shape
    vmem = pl.BlockSpec(memory_space=pltpu.VMEM)
    dma = pltpu.SemaphoreType.DMA
    return pl.pallas_call(
        reduce_kernel,
        out_shape=jax.ShapeDtypeStruct((depth // GROUPS, GROUPS * width), F32),
        in_specs=[vmem, vmem],
        out_specs=vmem,
        scratch_shapes=[
            pltpu.VMEM((n, depth, width), BF16),
            pltpu.VMEM((n - 1, depth, width), BF16),
            pltpu.VMEM((n - 1, depth, width), BF16),
            dma((n,)), dma((n,)), dma((n - 1,)), dma((n - 1,)),
        ],
        compiler_params=pltpu.CompilerParams(
            collective_id=1, has_side_effects=True, vmem_limit_bytes=VMEM_BYTES),
    )(fwd, tr)


def total_kernel(part_ref, out_ref, slots, send, recv):
    rows, cols = lax.axis_size("row"), lax.axis_size("col")
    count = rows * cols
    r, c = lax.axis_index("row"), lax.axis_index("col")
    me = r * cols + c
    barrier = pltpu.get_barrier_semaphore()

    def peer(d):
        other = lax.rem(me + d, count)
        return (other // cols, lax.rem(other, cols))

    def greet(d, _):
        pl.semaphore_signal(barrier, inc=1, device_id=peer(d), device_id_type=MESH)
        return 0
    lax.fori_loop(1, count, greet, 0)
    slots[me] = part_ref[...]
    pl.semaphore_wait(barrier, count - 1)

    def copy(d):
        return pltpu.make_async_remote_copy(
            src_ref=part_ref, dst_ref=slots.at[me],
            send_sem=send.at[d], recv_sem=recv.at[d],
            device_id=peer(d), device_id_type=MESH)

    def start(d, _):
        copy(d).start()
        return 0

    def finish(d, _):
        copy(d).wait()
        return 0
    lax.fori_loop(1, count, start, 0)
    lax.fori_loop(1, count, finish, 0)
    out_ref[...] = jnp.sum(slots[...], axis=0)


def total_over_devices(part, count):
    vmem = pl.BlockSpec(memory_space=pltpu.VMEM)
    dma = pltpu.SemaphoreType.DMA
    return pl.pallas_call(
        total_kernel,
        out_shape=jax.ShapeDtypeStruct(part.shape, F32),
        in_specs=[vmem],
        out_specs=vmem,
        scratch_shapes=[pltpu.VMEM((count,) + part.shape, F32), dma((count,)), dma((count,))],
        compiler_params=pltpu.CompilerParams(
            collective_id=2, has_side_effects=True, vmem_limit_bytes=VMEM_BYTES),
    )(part)


def body(x_vec, hx_vec, p_vec, hp_vec, theta, precond, tile_vals, tile_rows, tile_cols, tile_count):
    vec_count, piece_len = x_vec.shape
    row_count = lax.axis_size("row")
    col_count = lax.axis_size("col")
    ndim_total = piece_len * row_count * col_count
    residue = (hx_vec - x_vec * theta[:, None]) / precond[None, :]
    width = piece_len // GROUPS
    w_send = residue.astype(BF16).reshape(vec_count, GROUPS, width)
    w_send = jnp.transpose(w_send, (1, 0, 2)).reshape(GROUPS * vec_count, width)
    slot_total = tile_vals.shape[2]
    vals = tile_vals.reshape(slot_total * BLOCK * BLOCK // 128, 128)
    own, far = gather_pieces(w_send, row_count)
    fwd, tr = block_products(vals, tile_rows[0, 0], tile_cols[0, 0], tile_count[0], own, far)
    hw_vec = reduce_pieces(fwd, tr)
    vectors = jnp.concatenate([x_vec, residue, p_vec], 0)
    images = jnp.concatenate([hx_vec, hw_vec, hp_vec], 0)
    dims = (((1,), (1,)), ((), ()))
    local_a = lax.dot_general(vectors, images, dims, precision=lax.Precision.HIGHEST,
                              preferred_element_type=F32)
    local_b = lax.dot_general(vectors, vectors, dims, precision=lax.Precision.HIGHEST,
                              preferred_element_type=F32)
    rows = vectors.shape[0]
    part = jnp.zeros((32, 128), F32).at[:rows, :rows].set(local_a).at[16:16 + rows, :rows].set(local_b)
    total = total_over_devices(part, row_count * col_count) / ndim_total
    return (hw_vec, total[:rows, :rows], total[16:16 + rows, :rows])


def solution(mesh):
    placed = (
        P(None, ("col", "row")),
        P(None, ("col", "row")),
        P(None, ("col", "row")),
        P(None, ("col", "row")),
        P(),
        P(("col", "row")),
        P("row", "col", None, None),
        P("row", "col", None),
        P("row", "col", None),
        P("row", "col"),
    )
    return jax.shard_map(
        body,
        mesh=mesh,
        in_specs=placed,
        out_specs=(P(None, ("col", "row")), P(), P()),
        check_vma=False,
    )
```

time: 893 us -> 133 us (0.15)
  the two profiles are of different devices: /device:TPU:0 before, /device:TPU:13 now
where the time goes in v1:
time: 133 us; the launch traced here: 131 us
  Pallas kernels  106 us (80%)
  local copies, waits for them, and re-layouts  17.5 us (13%)
  matrix products  4.07 us (3%)
  other arithmetic  1.96 us (1%)
  between operations  1.46 us (1%)
    pallas_call x1, Pallas kernels, block_products(): pl.pallas_call(functools.partial(product_kernel, chunk), out_shape=(jax.S...  41.1 us
    pallas_call x1, Pallas kernels, reduce_pieces(): pl.pallas_call(reduce_kernel, out_shape=jax.ShapeDtypeStruct((depth // GR...  29.5 us
    pallas_call x1, Pallas kernels, total_over_devices(): pl.pallas_call(total_kernel, out_shape=jax.ShapeDtypeStruct(part.shape, F...  18.4 us
    pallas_call x1, Pallas kernels, gather_pieces(): pl.pallas_call(gather_kernel, out_shape=(shape, shape), in_specs=[vmem],...  17.4 us
    reshape x1, local copies, waits for them, and re-layouts, body(): vals = tile_vals.reshape(slot_total * BLOCK * BLOCK // 128, 128)  13.5 us

profile of v1, /device:TPU:13, one launch (start us, length us, event | category | flops | bytes accessed | tf_op | source)
XLA Modules:
  0.0 131.3 jit_solution(12664171948217962810)
XLA Ops:
  0.6 1.2 fusion.9
  1.9 0.7 reshape.80.w_ref
  2.6 17.4 %shard_map.121 = (bf16[4,16,4096]{2,1,0:T(8,128)(2,1)}, bf16[4,16,4096]{2,1,0:T(8,128)(2,1)}) custom-call(bf16[16,4096]{1,0:T(8,128)(2,1)} %reshape.80.w_ref), custom_call_target="tpu_custom_call" | custom-call | tf_op jit(solution)/shard_map/pallas_call | solution.py:111
  20.0 13.5 %reshape.78.vals_ref = bf16[32768,128]{1,0:T(8,128)(2,1)} reshape(bf16[1,1,1024,4096]{3,2,1,0:T(8,128)(2,1)} %param.20) | data formatting | bytes 16777216 | tf_op jit(solution)/shard_map/reshape | solution.py:400
  33.5 0.0 copy-start
  33.5 0.0 copy-start.1
  33.5 0.0 copy-start.3
  33.5 0.0 copy-start.4
  34.2 41.1 %shard_map.122 = (bf16[4,16,4096]{2,1,0:T(8,128)(2,1)}, f32[4,16,4096]{2,1,0:T(8,128)}) custom-call(s32[1024]{0:T(1024)} %bitcast.10, s32[1024]{0:T(1024)} %bitcast.11, s32[1]{0:T(128)} %bitcast.8.count_ref, bf16[32768,128]{1,0:T(8,128)(2,1)} %reshape.78.vals_ref, bf16[4,16,4096]{2,1,0:T(8,128)(2,1)} %get-tuple-element.31.own_ref, ...), custom_call_target="tpu_custom_call" | custom-call | tf_op jit(solution)/shard_map/pallas_call | solution.py:240
  75.3 29.5 %shard_map.123 = f32[4,16384]{1,0:T(4,128)} custom-call(bf16[4,16,4096]{2,1,0:T(8,128)(2,1)} %get-tuple-element.33.fwd_ref, f32[4,16,4096]{2,1,0:T(8,128)} %get-tuple-element.34.tr_ref), custom_call_target="tpu_custom_call" | custom-call | tf_op jit(solution)/shard_map/pallas_call | solution.py:324
  104.8 0.0 copy-done
  104.8 0.0 copy-done.1
  104.8 0.0 copy-done.3
  104.8 0.0 copy-done.4
  104.8 2.5 %fusion = f32[12,12]{1,0:T(8,128)S(1)} fusion(f32[4,16384]{1,0:T(4,128)S(1)} %copy-done.3, f32[4,16384]{1,0:T(4,128)} %shard_map.123, f32[4,16384]{1,0:T(4,128)S(1)} %copy-done, f32[4,16384]{1,0:T(4,128)S(1)} %copy-done.4, f32[4,16384]{1,0:T(4,128)S(1)} %get-tuple-element.36, f32[4,16384]{1,0:T(4,128)S(1)} %copy-done.1), kind=kOutput, calls=%fused_computation.1 | convolution fusion | flops 29097984 | bytes 1573440 | tf_op jit(solution)/shard_map/dot_general | solution.py:407
  107.3 1.6 %fusion.6 = f32[12,12]{1,0:T(8,128)S(1)} fusion(f32[4,16384]{1,0:T(4,128)S(1)} %copy-done.4, f32[4,16384]{1,0:T(4,128)S(1)} %get-tuple-element.36, f32[4,16384]{1,0:T(4,128)S(1)} %copy-done.1), kind=kOutput, calls=%fused_computation.7 | convolution fusion | flops 28704768 | bytes 787008 | tf_op jit(solution)/shard_map/dot_general | solution.py:409
  108.9 0.4 scatter.9.part_ref
  109.3 0.0 copy-start.2
  109.4 0.6 copy-done.2
  109.9 18.4 %shard_map.124 = f32[32,128]{1,0:T(8,128)} custom-call(f32[32,128]{1,0:T(8,128)} %copy-done.2), custom_call_target="tpu_custom_call" | custom-call | tf_op jit(solution)/shard_map/pallas_call | solution.py:379
  128.3 0.7 broadcast_multiply_fusion
  129.0 0.6 fusion.10
  129.7 1.7 %copy.17 = f32[4,16384]{1,0:T(4,128)} copy(f32[4,16384]{1,0:T(4,128)} %shard_map.123) | data formatting | bytes 524288
  (1 shorter events, 0.0 us)
Async XLA Ops:
  33.5 71.3 %copy-start = (f32[4,16384]{1,0:T(4,128)S(1)}, f32[4,16384]{1,0:T(4,128)}, u32[]{:S(2)}) copy-start(f32[4,16384]{1,0:T(4,128)} %param.15) | copy-start | bytes 786436
  33.5 71.3 %copy-start.1 = (f32[4,16384]{1,0:T(4,128)S(1)}, f32[4,16384]{1,0:T(4,128)}, u32[]{:S(2)}) copy-start(f32[4,16384]{1,0:T(4,128)} %param.14) | copy-start | bytes 786436
  33.5 71.3 %copy-start.3 = (f32[4,16384]{1,0:T(4,128)S(1)}, f32[4,16384]{1,0:T(4,128)}, u32[]{:S(2)}) copy-start(f32[4,16384]{1,0:T(4,128)} %param.17) | copy-start | bytes 786436
  33.5 71.3 %copy-start.4 = (f32[4,16384]{1,0:T(4,128)S(1)}, f32[4,16384]{1,0:T(4,128)}, u32[]{:S(2)}) copy-start(f32[4,16384]{1,0:T(4,128)} %param.16) | copy-start | bytes 786436
  109.3 0.6 copy-start.2

commit v2 on v1

--- a/solution.py
+++ b/solution.py
@@ -120,7 +120,7 @@
 
 
 def product_kernel(chunk, rows_ref, cols_ref, count_ref, vals_ref, own_ref, far_ref, fwd_ref, tr_ref,
-                   x_col, x_row, acc_f, acc_t):
+                   x_col, x_row, acc_f, acc_t, loose, packed):
     step, steps = pl.program_id(0), pl.num_programs(0)
     n, _, width = own_ref.shape
     tiles = width // 128
@@ -130,13 +130,21 @@
     left = lane_iota() < 64
     keep = low == left
     quarter = lane_iota() // 32
+    batch = min(tiles, 16)
+
+    def each_tile(visit):
+        def some(i, _):
+            q, t0 = i // (tiles // batch), (i % (tiles // batch)) * batch
+            for t in range(batch):
+                visit(q, t0 + t)
+            return 0
+        lax.fori_loop(0, n * tiles // batch, some, 0)
 
     def block_at(q, g, t, parity):
         return q * (GROUPS * per_group) + g * per_group + 2 * t + parity
 
     def expand(src_ref, dst_ref):
-        def tile(i, _):
-            q, t = i // tiles, i % tiles
+        def tile(q, t):
             s = src_ref[q, :, pl.ds(pl.multiple_of(t * 128, 128), 128)].astype(F32)
             for h in range(2):
                 v = s[8 * h:8 * h + 8]
@@ -147,8 +155,9 @@
                 dst_ref[block_at(q, 2 * h, t, 1)] = jnp.where(keep, jnp.where(low, vl, vs), 0.0)
                 dst_ref[block_at(q, 2 * h + 1, t, 0)] = jnp.where(keep, jnp.where(low, vs, vl), 0.0)
                 dst_ref[block_at(q, 2 * h + 1, t, 1)] = jnp.where(keep, jnp.where(low, vls, v), 0.0)
-            return 0
-        lax.fori_loop(0, n * tiles, tile, 0, unroll=4)
+        each_tile(tile)
+
+    part_size = 64
 
     @pl.when(step == 0)
     def _():
@@ -157,23 +166,31 @@
         spread = spread_matrix()
 
         def part(i, _):
-            at = pl.ds(i * 32, 32)
-            x = x_row[at].reshape(256, 128).astype(BF16)
-            x_row[at] = jnp.dot(x, spread, preferred_element_type=F32).reshape(32, 8, 128)
-            zero = jnp.zeros((32, 8, 128), F32)
+            at = pl.ds(i * part_size, part_size)
+            x = x_row[at].reshape(part_size * 8, 128).astype(BF16)
+            x_row[at] = jnp.dot(x, spread, preferred_element_type=F32).reshape(part_size, 8, 128)
+            zero = jnp.zeros((part_size, 8, 128), F32)
             acc_f[at] = zero
             acc_t[at] = zero
             return 0
-        lax.fori_loop(0, nblk // 32, part, 0)
+        lax.fori_loop(0, nblk // part_size, part, 0)
 
     count = count_ref[0]
     first = step * chunk
     live = jnp.clip(count - first, 0, chunk)
 
-    def octet(i, _):
-        for half in range(2):
-            at = i * 8 + half * 4
-            w = vals_ref[pl.ds(pl.multiple_of(at * 32, 128), 128), :]
+    def retile(i, _):
+        for s in range(32):
+            v = vals_ref[pl.ds(pl.multiple_of(i * 16, 16), 16), s * 128:(s + 1) * 128]
+            loose[pl.ds(s, 16, stride=32), :] = v.astype(F32)
+        packed[pl.ds(pl.multiple_of(i * 512, 512), 512), :] = loose[...].astype(BF16)
+        return 0
+    lax.fori_loop(0, (live + 15) // 16, retile, 0)
+
+    def some_slots(i, _):
+        for part in range(4):
+            at = i * 16 + part * 4
+            w = packed[pl.ds(pl.multiple_of(at * 32, 128), 128), :]
             rows, cols, lf, lt = [], [], [], []
             for z in range(4):
                 slot = first + at + z
@@ -190,42 +207,36 @@
                 acc_f[rows[z]] += jnp.where(quarter == z, of[8 * z:8 * z + 8], 0.0)
                 acc_t[cols[z]] += ot[8 * z:8 * z + 8]
         return 0
-    lax.fori_loop(0, (live + 7) // 8, octet, 0)
+    lax.fori_loop(0, (live + 15) // 16, some_slots, 0)
 
     @pl.when(step == steps - 1)
     def _():
         spread = spread_matrix()
 
         def part(i, _):
-            at = pl.ds(i * 32, 32)
-            x = acc_f[at].reshape(256, 128)
+            at = pl.ds(i * part_size, part_size)
+            x = acc_f[at].reshape(part_size * 8, 128)
             hi = x.astype(BF16)
             lo = (x - hi.astype(F32)).astype(BF16)
             back = (((1,), (1,)), ((), ()))
             y = lax.dot_general(hi, spread, back, preferred_element_type=F32)
             y += lax.dot_general(lo, spread, back, preferred_element_type=F32)
-            acc_f[at] = y.reshape(32, 8, 128)
+            acc_f[at] = y.reshape(part_size, 8, 128)
             return 0
-        lax.fori_loop(0, nblk // 32, part, 0)
+        lax.fori_loop(0, nblk // part_size, part, 0)
 
         def fold(src_ref, dst_ref):
-            def folded(q, g, t, parity):
-                x = jnp.where(keep, src_ref[block_at(q, g, t, parity)], 0.0)
-                return x + pltpu.roll(pltpu.roll(x, 64, 1), 4, 0)
-
-            def tile(i, _):
-                q, t = i // tiles, i % tiles
+            def tile(q, t):
                 out = []
                 for h in range(2):
-                    e0, o0 = folded(q, 2 * h, t, 0), folded(q, 2 * h, t, 1)
-                    e1, o1 = folded(q, 2 * h + 1, t, 0), folded(q, 2 * h + 1, t, 1)
-                    top = jnp.where(left, e0, pltpu.roll(o0, 4, 0))
-                    bottom = jnp.where(left, pltpu.roll(e1, 4, 0), o1)
-                    out.append(jnp.where(low, top, bottom))
+                    e0, o0 = src_ref[block_at(q, 2 * h, t, 0)], src_ref[block_at(q, 2 * h, t, 1)]
+                    e1, o1 = src_ref[block_at(q, 2 * h + 1, t, 0)], src_ref[block_at(q, 2 * h + 1, t, 1)]
+                    stay = jnp.where(keep, jnp.where(low, e0, o1), pltpu.roll(jnp.where(low, o0, e1), 64, 1))
+                    move = jnp.where(keep, jnp.where(low, e1, o0), pltpu.roll(jnp.where(low, o1, e0), 64, 1))
+                    out.append(stay + pltpu.roll(move, 4, 0))
                 at = pl.ds(pl.multiple_of(t * 128, 128), 128)
                 dst_ref[q, :, at] = jnp.concatenate(out, 0).astype(dst_ref.dtype)
-                return 0
-            lax.fori_loop(0, n * tiles, tile, 0, unroll=4)
+            each_tile(tile)
 
         fold(acc_f, fwd_ref)
         fold(acc_t, tr_ref)
@@ -233,7 +244,7 @@
 
 def block_products(vals, rows, cols, count, own, far):
     slots = rows.shape[0]
-    chunk = 64
+    chunk = 128
     n, depth, width = own.shape
     nblk = n * GROUPS * (width // 64)
     whole = pl.BlockSpec((n, depth, width), lambda i, *_: (0, 0, 0))
@@ -243,13 +254,15 @@
         grid_spec=pltpu.PrefetchScalarGridSpec(
             num_scalar_prefetch=3,
             grid=(slots // chunk,),
-            in_specs=[pl.BlockSpec((chunk * 32, 128), lambda i, *_: (i, 0)), whole, whole],
+            in_specs=[pl.BlockSpec((chunk, vals.shape[1]), lambda i, *_: (i, 0)), whole, whole],
             out_specs=(whole, whole),
             scratch_shapes=[
                 pltpu.VMEM((nblk, 8, 128), F32),
                 pltpu.VMEM((nblk, 8, 128), F32),
                 pltpu.VMEM((nblk + 1, 8, 128), F32),
                 pltpu.VMEM((nblk + 1, 8, 128), F32),
+                pltpu.VMEM((512, 128), F32),
+                pltpu.VMEM((chunk * 32, 128), BF16),
             ],
         ),
         compiler_params=pltpu.CompilerParams(vmem_limit_bytes=VMEM_BYTES),
@@ -396,10 +409,8 @@
     width = piece_len // GROUPS
     w_send = residue.astype(BF16).reshape(vec_count, GROUPS, width)
     w_send = jnp.transpose(w_send, (1, 0, 2)).reshape(GROUPS * vec_count, width)
-    slot_total = tile_vals.shape[2]
-    vals = tile_vals.reshape(slot_total * BLOCK * BLOCK // 128, 128)
     own, far = gather_pieces(w_send, row_count)
-    fwd, tr = block_products(vals, tile_rows[0, 0], tile_cols[0, 0], tile_count[0], own, far)
+    fwd, tr = block_products(tile_vals[0, 0], tile_rows[0, 0], tile_cols[0, 0], tile_count[0], own, far)
     hw_vec = reduce_pieces(fwd, tr)
     vectors = jnp.concatenate([x_vec, residue, p_vec], 0)
     images = jnp.concatenate([hx_vec, hw_vec, hp_vec], 0)

time: 133 us -> 110 us (0.83)
  the two profiles are of different devices: /device:TPU:13 before, /device:TPU:15 now
where the time goes in v2:
time: 110 us; the launch traced here: 109 us
  Pallas kernels  97.9 us (89%)
  matrix products  4.07 us (4%)
  local copies, waits for them, and re-layouts  4.02 us (4%)
  other arithmetic  2.04 us (2%)
  between operations  1.4 us (1%)
    pallas_call x1, Pallas kernels, block_products(): pl.pallas_call(functools.partial(product_kernel, chunk), out_shape=(jax.S...  40.5 us
    pallas_call x1, Pallas kernels, reduce_pieces(): pl.pallas_call(reduce_kernel, out_shape=jax.ShapeDtypeStruct((depth // GR...  20.7 us
    pallas_call x1, Pallas kernels, total_over_devices(): pl.pallas_call(total_kernel, out_shape=jax.ShapeDtypeStruct(part.shape, F...  19.2 us
    pallas_call x1, Pallas kernels, gather_pieces(): pl.pallas_call(gather_kernel, out_shape=(shape, shape), in_specs=[vmem],...  17.4 us
    dot_general x1, matrix products, body(): lax.dot_general(vectors, images, dims, precision=lax.Precision.HIGHEST, p...  2.51 us
    unnamed x11, local copies, waits for them, and re-layouts  2.29 us

profile of v2, /device:TPU:15, one launch (start us, length us, event | category | flops | bytes accessed | tf_op | source)
XLA Modules:
  0.0 109.4 jit_solution(16213613269226381785)
XLA Ops:
  0.6 0.0 copy-start.1
  0.6 0.0 copy-start
  0.7 0.0 copy-start.4
  0.7 0.0 copy-start.3
  0.7 1.3 %fusion.9 = (bf16[4,16384]{1,0:T(4,128)(2,1)S(1)}, f32[4,16384]{1,0:T(4,128)S(1)}) fusion(f32[16384]{0:T(1024)} %param.19, f32[4,16384]{1,0:T(4,128)} %param.15, f32[4,16384]{1,0:T(4,128)} %param.14, f32[4]{0:T(128)} %param.18), kind=kLoop, calls=%fused_computation.12 | loop fusion | flops 262144 | bytes 983056 | tf_op jit(solution)/shard_map/convert_element_type | solution.py:410
  2.0 0.7 reshape.76.w_ref
  2.7 17.4 %shard_map.121 = (bf16[4,16,4096]{2,1,0:T(8,128)(2,1)}, bf16[4,16,4096]{2,1,0:T(8,128)(2,1)}) custom-call(bf16[16,4096]{1,0:T(8,128)(2,1)} %reshape.76.w_ref), custom_call_target="tpu_custom_call" | custom-call | tf_op jit(solution)/shard_map/pallas_call | solution.py:111
  20.8 40.5 %shard_map.122 = (bf16[4,16,4096]{2,1,0:T(8,128)(2,1)}, f32[4,16,4096]{2,1,0:T(8,128)}) custom-call(s32[1024]{0:T(1024)} %bitcast.10, s32[1024]{0:T(1024)} %bitcast.11, s32[1]{0:T(128)} %bitcast.7.count_ref, bf16[1024,4096]{1,0:T(8,128)(2,1)} %bitcast.8, bf16[4,16,4096]{2,1,0:T(8,128)(2,1)} %get-tuple-element.31.own_ref, ...), custom_call_target="tpu_custom_call" | custom-call | tf_op jit(solution)/shard_map/pallas_call | solution.py:251
  61.3 20.7 %shard_map.123 = f32[4,16384]{1,0:T(4,128)} custom-call(bf16[4,16,4096]{2,1,0:T(8,128)(2,1)} %get-tuple-element.33.fwd_ref, f32[4,16,4096]{2,1,0:T(8,128)} %get-tuple-element.34.tr_ref), custom_call_target="tpu_custom_call" | custom-call | tf_op jit(solution)/shard_map/pallas_call | solution.py:337
  82.0 0.0 copy-done.1
  82.0 0.0 copy-done
  82.1 0.0 copy-done.4
  82.1 0.0 copy-done.3
  82.1 2.5 %fusion = f32[12,12]{1,0:T(8,128)S(1)} fusion(f32[4,16384]{1,0:T(4,128)S(1)} %copy-done.3, f32[4,16384]{1,0:T(4,128)} %shard_map.123, f32[4,16384]{1,0:T(4,128)S(1)} %copy-done, f32[4,16384]{1,0:T(4,128)S(1)} %copy-done.4, f32[4,16384]{1,0:T(4,128)S(1)} %get-tuple-element.36, f32[4,16384]{1,0:T(4,128)S(1)} %copy-done.1), kind=kOutput, calls=%fused_computation.1 | convolution fusion | flops 29097984 | bytes 1573440 | tf_op jit(solution)/shard_map/dot_general | solution.py:418
  84.6 1.6 %fusion.6 = f32[12,12]{1,0:T(8,128)S(1)} fusion(f32[4,16384]{1,0:T(4,128)S(1)} %copy-done.4, f32[4,16384]{1,0:T(4,128)S(1)} %get-tuple-element.36, f32[4,16384]{1,0:T(4,128)S(1)} %copy-done.1), kind=kOutput, calls=%fused_computation.7 | convolution fusion | flops 28704768 | bytes 787008 | tf_op jit(solution)/shard_map/dot_general | solution.py:420
  86.2 0.4 scatter.9.part_ref
  86.6 0.0 copy-start.2
  86.6 0.6 copy-done.2
  87.2 19.2 %shard_map.124 = f32[32,128]{1,0:T(8,128)} custom-call(f32[32,128]{1,0:T(8,128)} %copy-done.2), custom_call_target="tpu_custom_call" | custom-call | tf_op jit(solution)/shard_map/pallas_call | solution.py:392
  106.4 0.7 broadcast_multiply_fusion
  107.2 0.6 fusion.10
  107.8 1.7 %copy.17 = f32[4,16384]{1,0:T(4,128)} copy(f32[4,16384]{1,0:T(4,128)} %shard_map.123) | data formatting | bytes 524288
  (1 shorter events, 0.0 us)
Async XLA Ops:
  0.6 81.4 %copy-start.1 = (f32[4,16384]{1,0:T(4,128)S(1)}, f32[4,16384]{1,0:T(4,128)}, u32[]{:S(2)}) copy-start(f32[4,16384]{1,0:T(4,128)} %param.14) | copy-start | bytes 786436
  0.6 81.4 %copy-start = (f32[4,16384]{1,0:T(4,128)S(1)}, f32[4,16384]{1,0:T(4,128)}, u32[]{:S(2)}) copy-start(f32[4,16384]{1,0:T(4,128)} %param.15) | copy-start | bytes 786436
  0.7 81.4 %copy-start.4 = (f32[4,16384]{1,0:T(4,128)S(1)}, f32[4,16384]{1,0:T(4,128)}, u32[]{:S(2)}) copy-start(f32[4,16384]{1,0:T(4,128)} %param.16) | copy-start | bytes 786436
  0.7 81.4 %copy-start.3 = (f32[4,16384]{1,0:T(4,128)S(1)}, f32[4,16384]{1,0:T(4,128)}, u32[]{:S(2)}) copy-start(f32[4,16384]{1,0:T(4,128)} %param.17) | copy-start | bytes 786436
  86.6 0.6 copy-start.2

commit v3 on v2

--- a/solution.py
+++ b/solution.py
@@ -269,20 +269,21 @@
     )(rows, cols, count, vals, own, far)
 
 
-def reduce_kernel(fwd_ref, tr_ref, out_ref, far, stage, landed, far_send, far_recv, send, recv):
+def reduce_kernel(fwd_ref, tr_ref, x_ref, res_ref, p_ref, hx_ref, hp_ref, out_ref, a_ref, b_ref,
+                  far, stage, landed, part, half, col_slots, row_slots,
+                  far_send, far_recv, send, recv, col_send, col_recv, row_send, row_recv):
     n = fwd_ref.shape[0]
+    vecs, length = x_ref.shape
+    basis = 3 * vecs
     cols = lax.axis_size("col")
     r, c = lax.axis_index("row"), lax.axis_index("col")
     target = lax.rem(c + r, cols)
-    source = lax.rem(c - r + cols, cols)
     barrier = pltpu.get_barrier_semaphore()
     for d in range(1, n):
         pl.semaphore_signal(barrier, inc=1, device_id=(lax.rem(r + d, n), c), device_id_type=MESH)
-
-    @pl.when(r > 0)
-    def _():
-        pl.semaphore_signal(barrier, inc=1, device_id=(r, source), device_id_type=MESH)
-    pl.semaphore_wait(barrier, jnp.where(r > 0, n, n - 1))
+    for d in range(1, cols):
+        pl.semaphore_signal(barrier, inc=1, device_id=(r, lax.rem(c + d, cols)), device_id_type=MESH)
+    pl.semaphore_wait(barrier, n + cols - 2)
 
     def far_copy(d):
         q = lax.rem(r + d, n)
@@ -297,6 +298,31 @@
             send_sem=send.at[d - 1], recv_sem=recv.at[d - 1],
             device_id=(lax.rem(r + d, n), c), device_id_type=MESH)
 
+    def col_sum_copy(d):
+        return pltpu.make_async_remote_copy(
+            src_ref=part, dst_ref=col_slots.at[c],
+            send_sem=col_send.at[d], recv_sem=col_recv.at[d],
+            device_id=(r, lax.rem(c + d, cols)), device_id_type=MESH)
+
+    def row_sum_copy(d):
+        return pltpu.make_async_remote_copy(
+            src_ref=half, dst_ref=row_slots.at[r],
+            send_sem=row_send.at[d], recv_sem=row_recv.at[d],
+            device_id=(lax.rem(r + d, n), c), device_id_type=MESH)
+
+    def products(left_refs, right_refs):
+        span = min(length, 2048)
+        height = len(left_refs) * vecs
+        across = len(right_refs) * vecs
+
+        def some(i, total):
+            at = pl.ds(pl.multiple_of(i * span, span), span)
+            v = jnp.concatenate([ref[:, at] for ref in left_refs], 0)
+            w = jnp.concatenate([ref[:, at] for ref in right_refs], 0)
+            return total + lax.dot_general(v, w, (((1,), (1,)), ((), ())), precision=lax.Precision.HIGHEST,
+                                           preferred_element_type=F32)
+        return lax.fori_loop(0, length // span, some, jnp.zeros((height, across), F32))
+
     order = list(range(1, n)) + [0]
 
     @pl.when(r > 0)
@@ -307,6 +333,10 @@
     @pl.when(r == 0)
     def _():
         far[...] = fwd_ref[...]
+
+    part[...] = jnp.zeros_like(part)
+    left = [x_ref, res_ref, p_ref]
+    part[:basis, :5 * vecs] = products(left, left + [hx_ref, hp_ref])
 
     for d in order:
         pl.when(r > 0)(lambda: far_copy(d).wait_recv())
@@ -321,8 +351,30 @@
     width = total.shape[1]
     for g in range(GROUPS):
         out_ref[:, g * width:(g + 1) * width] = total[4 * g:4 * g + 4]
+
+    part[:basis, 5 * vecs:6 * vecs] = products(left, [out_ref])
+    for d in range(1, cols):
+        col_sum_copy(d).start()
+    col_slots[c] = part[...]
+    for d in range(1, cols):
+        col_sum_copy(d).wait_recv()
+    half[...] = jnp.sum(col_slots[...], axis=0)
+    for d in range(1, n):
+        row_sum_copy(d).start()
+    row_slots[r] = half[...]
+    for d in range(1, n):
+        row_sum_copy(d).wait_recv()
+    gram = jnp.sum(row_slots[...], axis=0) * (1.0 / (length * n * cols))
+    b_ref[...] = gram[:basis, :basis]
+    a_ref[:, :vecs] = gram[:basis, 3 * vecs:4 * vecs]
+    a_ref[:, vecs:2 * vecs] = gram[:basis, 5 * vecs:6 * vecs]
+    a_ref[:, 2 * vecs:] = gram[:basis, 4 * vecs:5 * vecs]
+
     for d in range(1, n):
         row_copy(d).wait_send()
+        row_sum_copy(d).wait_send()
+    for d in range(1, cols):
+        col_sum_copy(d).wait_send()
 
     @pl.when(r > 0)
     def _():
@@ -330,99 +382,45 @@
             far_copy(d).wait_send()
 
 
-def reduce_pieces(fwd, tr):
+def reduce_pieces(fwd, tr, x_vec, residue, p_vec, hx_vec, hp_vec, cols):
     n, depth, width = fwd.shape
+    basis = 3 * x_vec.shape[0]
     vmem = pl.BlockSpec(memory_space=pltpu.VMEM)
     dma = pltpu.SemaphoreType.DMA
+    small = (16, 128)
+    gram = jax.ShapeDtypeStruct((basis, basis), F32)
     return pl.pallas_call(
         reduce_kernel,
-        out_shape=jax.ShapeDtypeStruct((depth // GROUPS, GROUPS * width), F32),
-        in_specs=[vmem, vmem],
-        out_specs=vmem,
+        out_shape=(jax.ShapeDtypeStruct(x_vec.shape, F32), gram, gram),
+        in_specs=[vmem] * 7,
+        out_specs=(vmem,) * 3,
         scratch_shapes=[
             pltpu.VMEM((n, depth, width), BF16),
             pltpu.VMEM((n - 1, depth, width), BF16),
             pltpu.VMEM((n - 1, depth, width), BF16),
+            pltpu.VMEM(small, F32),
+            pltpu.VMEM(small, F32),
+            pltpu.VMEM((cols,) + small, F32),
+            pltpu.VMEM((n,) + small, F32),
             dma((n,)), dma((n,)), dma((n - 1,)), dma((n - 1,)),
+            dma((cols,)), dma((cols,)), dma((n,)), dma((n,)),
         ],
         compiler_params=pltpu.CompilerParams(
             collective_id=1, has_side_effects=True, vmem_limit_bytes=VMEM_BYTES),
-    )(fwd, tr)
-
-
-def total_kernel(part_ref, out_ref, slots, send, recv):
-    rows, cols = lax.axis_size("row"), lax.axis_size("col")
-    count = rows * cols
-    r, c = lax.axis_index("row"), lax.axis_index("col")
-    me = r * cols + c
-    barrier = pltpu.get_barrier_semaphore()
-
-    def peer(d):
-        other = lax.rem(me + d, count)
-        return (other // cols, lax.rem(other, cols))
-
-    def greet(d, _):
-        pl.semaphore_signal(barrier, inc=1, device_id=peer(d), device_id_type=MESH)
-        return 0
-    lax.fori_loop(1, count, greet, 0)
-    slots[me] = part_ref[...]
-    pl.semaphore_wait(barrier, count - 1)
-
-    def copy(d):
-        return pltpu.make_async_remote_copy(
-            src_ref=part_ref, dst_ref=slots.at[me],
-            send_sem=send.at[d], recv_sem=recv.at[d],
-            device_id=peer(d), device_id_type=MESH)
-
-    def start(d, _):
-        copy(d).start()
-        return 0
-
-    def finish(d, _):
-        copy(d).wait()
-        return 0
-    lax.fori_loop(1, count, start, 0)
-    lax.fori_loop(1, count, finish, 0)
-    out_ref[...] = jnp.sum(slots[...], axis=0)
-
-
-def total_over_devices(part, count):
-    vmem = pl.BlockSpec(memory_space=pltpu.VMEM)
-    dma = pltpu.SemaphoreType.DMA
-    return pl.pallas_call(
-        total_kernel,
-        out_shape=jax.ShapeDtypeStruct(part.shape, F32),
-        in_specs=[vmem],
-        out_specs=vmem,
-        scratch_shapes=[pltpu.VMEM((count,) + part.shape, F32), dma((count,)), dma((count,))],
-        compiler_params=pltpu.CompilerParams(
-            collective_id=2, has_side_effects=True, vmem_limit_bytes=VMEM_BYTES),
-    )(part)
+    )(fwd, tr, x_vec, residue, p_vec, hx_vec, hp_vec)
 
 
 def body(x_vec, hx_vec, p_vec, hp_vec, theta, precond, tile_vals, tile_rows, tile_cols, tile_count):
     vec_count, piece_len = x_vec.shape
     row_count = lax.axis_size("row")
     col_count = lax.axis_size("col")
-    ndim_total = piece_len * row_count * col_count
     residue = (hx_vec - x_vec * theta[:, None]) / precond[None, :]
     width = piece_len // GROUPS
     w_send = residue.astype(BF16).reshape(vec_count, GROUPS, width)
     w_send = jnp.transpose(w_send, (1, 0, 2)).reshape(GROUPS * vec_count, width)
     own, far = gather_pieces(w_send, row_count)
     fwd, tr = block_products(tile_vals[0, 0], tile_rows[0, 0], tile_cols[0, 0], tile_count[0], own, far)
-    hw_vec = reduce_pieces(fwd, tr)
-    vectors = jnp.concatenate([x_vec, residue, p_vec], 0)
-    images = jnp.concatenate([hx_vec, hw_vec, hp_vec], 0)
-    dims = (((1,), (1,)), ((), ()))
-    local_a = lax.dot_general(vectors, images, dims, precision=lax.Precision.HIGHEST,
-                              preferred_element_type=F32)
-    local_b = lax.dot_general(vectors, vectors, dims, precision=lax.Precision.HIGHEST,
-                              preferred_element_type=F32)
-    rows = vectors.shape[0]
-    part = jnp.zeros((32, 128), F32).at[:rows, :rows].set(local_a).at[16:16 + rows, :rows].set(local_b)
-    total = total_over_devices(part, row_count * col_count) / ndim_total
-    return (hw_vec, total[:rows, :rows], total[16:16 + rows, :rows])
+    return reduce_pieces(fwd, tr, x_vec, residue, p_vec, hx_vec, hp_vec, col_count)
 
 
 def solution(mesh):

time: 110 us -> 104 us (0.945)
  the two profiles are of different devices: /device:TPU:15 before, /device:TPU:0 now
where the time goes in v3:
time: 104 us; the launch traced here: 102 us
  Pallas kernels  93.6 us (90%)
  local copies, waits for them, and re-layouts  5.15 us (5%)
  other arithmetic  1.94 us (2%)
  between operations  1.31 us (1%)
    pallas_call x1, Pallas kernels, reduce_pieces(): pl.pallas_call(reduce_kernel, out_shape=(jax.ShapeDtypeStruct(x_vec.shape...  46.4 us
    pallas_call x1, Pallas kernels, block_products(): pl.pallas_call(functools.partial(product_kernel, chunk), out_shape=(jax.S...  26.2 us
    pallas_call x1, Pallas kernels, gather_pieces(): pl.pallas_call(gather_kernel, out_shape=(shape, shape), in_specs=[vmem],...  20.9 us
    unnamed x3, local copies, waits for them, and re-layouts  4.26 us

profile of v3, /device:TPU:0, one launch (start us, length us, event | category | flops | bytes accessed | tf_op | source)
XLA Modules:
  0.0 101.9 jit_solution(10745569112952138296)
XLA Ops:
  1.3 1.9 %fusion = (bf16[4,16384]{1,0:T(4,128)(2,1)S(1)}, f32[4,16384]{1,0:T(4,128)}) fusion(f32[16384]{0:T(1024)} %param.15, f32[4,16384]{1,0:T(4,128)} %hx_ref.1, f32[4,16384]{1,0:T(4,128)} %x_ref.1, f32[4]{0:T(128)} %param.14), kind=kLoop, calls=%fused_computation.1 | loop fusion | flops 262144 | bytes 983056 | tf_op jit(solution)/shard_map/convert_element_type | solution.py:419
  3.2 0.1 reshape.14
  3.3 0.1 copy.13
  3.4 0.7 reshape.15.w_ref
  4.1 20.9 %shard_map.121 = (bf16[4,16,4096]{2,1,0:T(8,128)(2,1)}, bf16[4,16,4096]{2,1,0:T(8,128)(2,1)}) custom-call(bf16[16,4096]{1,0:T(8,128)(2,1)} %reshape.15.w_ref), custom_call_target="tpu_custom_call" | custom-call | tf_op jit(solution)/shard_map/pallas_call | solution.py:111
  25.0 26.2 %shard_map.122 = (bf16[4,16,4096]{2,1,0:T(8,128)(2,1)}, f32[4,16,4096]{2,1,0:T(8,128)}) custom-call(s32[1024]{0:T(1024)} %bitcast.8, s32[1024]{0:T(1024)} %bitcast.9, s32[1]{0:T(128)} %bitcast.5.count_ref, bf16[1024,4096]{1,0:T(8,128)(2,1)} %bitcast.6, bf16[4,16,4096]{2,1,0:T(8,128)(2,1)} %get-tuple-element.7.own_ref, ...), custom_call_target="tpu_custom_call" | custom-call | tf_op jit(solution)/shard_map/pallas_call | solution.py:251
  51.2 46.4 %shard_map.123 = (f32[4,16384]{1,0:T(4,128)}, f32[12,12]{1,0:T(8,128)}, f32[12,12]{1,0:T(8,128)}) custom-call(bf16[4,16,4096]{2,1,0:T(8,128)(2,1)} %get-tuple-element.9.fwd_ref, f32[4,16,4096]{2,1,0:T(8,128)} %get-tuple-element.10.tr_ref, f32[4,16384]{1,0:T(4,128)} %x_ref.1, f32[4,16384]{1,0:T(4,128)} %get-tuple-element.12.res_ref, f32[4,16384]{1,0:T(4,128)} %p_ref.1, ...), custom_call_target="tpu_custom_call" | custom-call | tf_op jit(solution)/shard_map/pallas_call | solution.py:392
  97.7 1.7 %copy.18 = f32[4,16384]{1,0:T(4,128)} copy(f32[4,16384]{1,0:T(4,128)} %get-tuple-element.16) | data formatting | bytes 524288
  99.4 1.3 %copy.19 = f32[12,12]{1,0:T(8,128)} copy(f32[12,12]{1,0:T(8,128)} %get-tuple-element.17) | data formatting | bytes 1152
  100.7 1.3 %copy.20 = f32[12,12]{1,0:T(8,128)} copy(f32[12,12]{1,0:T(8,128)} %get-tuple-element.18) | data formatting | bytes 1152

commit v4 on v0

v4 whole, which is shorter than its diff:
```python
import functools
import jax
import jax.numpy as jnp
from jax import lax
from jax.experimental import pallas as pl
from jax.experimental.pallas import tpu as pltpu
from jax.sharding import PartitionSpec as P

BLOCK = 64
GROUPS = 4
CHUNK = 128
TOGETHER = 32
PART = 64
SMALL = (24, 128)
MESH = pl.DeviceIdType.MESH
F32 = jnp.float32
BF16 = jnp.bfloat16
VMEM_BYTES = 58 * 1024 * 1024


def row_iota():
    return lax.broadcasted_iota(jnp.int32, (8, 128), 0)


def lane_iota():
    return lax.broadcasted_iota(jnp.int32, (8, 128), 1)


def spread_matrix():
    a = lax.broadcasted_iota(jnp.int32, (128, 128), 0)
    b = lax.broadcasted_iota(jnp.int32, (128, 128), 1)
    return jnp.where((a % 64) == 2 * (b % 32) + a // 64, 1.0, 0.0).astype(BF16)


def gather_kernel(x_ref, hx_ref, p_ref, hp_ref, theta_ref, precond_ref, own_ref, res_ref, gram_ref,
                  up_send, up_recv, down_send, down_recv):
    n, _, width = own_ref.shape
    vecs, length = x_ref.shape
    r, c = lax.axis_index("row"), lax.axis_index("col")
    barrier = pltpu.get_barrier_semaphore()

    def greet(row):
        pl.semaphore_signal(barrier, inc=1, device_id=(row, c), device_id_type=MESH)

    pl.when(r > 0)(lambda: greet(r - 1))
    pl.when(r < n - 1)(lambda: greet(r + 1))
    which = lax.broadcasted_iota(jnp.int32, (vecs, 1), 0)
    theta = jnp.zeros((vecs, 1), F32)
    for k in range(vecs):
        theta = jnp.where(which == k, theta_ref[k], theta)
    for g in range(GROUPS):
        at = slice(g * width, (g + 1) * width)
        res_ref[:, at] = (hx_ref[:, at] - x_ref[:, at] * theta) / precond_ref[:, at]
    own_ref[r] = jnp.concatenate(
        [res_ref[:, g * width:(g + 1) * width] for g in range(GROUPS)], 0).astype(BF16)
    pl.semaphore_wait(barrier, jnp.where((r > 0) & (r < n - 1), 2, 1))

    def up_copy(piece, d):
        return pltpu.make_async_remote_copy(
            src_ref=own_ref.at[piece], dst_ref=own_ref.at[piece],
            send_sem=up_send.at[d], recv_sem=up_recv.at[d],
            device_id=(r + 1, c), device_id_type=MESH)

    def down_copy(piece, d):
        return pltpu.make_async_remote_copy(
            src_ref=own_ref.at[piece], dst_ref=own_ref.at[piece],
            send_sem=down_send.at[d], recv_sem=down_recv.at[d],
            device_id=(r - 1, c), device_id_type=MESH)

    span = min(length, 2048)
    spans = length // span
    each = -(-spans // (n - 1))
    left = [x_ref, res_ref, p_ref]
    right = left + [hx_ref, hp_ref]

    def some(i, total):
        at = pl.ds(pl.multiple_of(i * span, span), span)
        v = jnp.concatenate([ref[:, at] for ref in left], 0)
        w = jnp.concatenate([ref[:, at] for ref in right], 0)
        return total + lax.dot_general(v, w, (((1,), (1,)), ((), ())), precision=lax.Precision.HIGHEST,
                                       preferred_element_type=F32)

    pl.when(r < n - 1)(lambda: up_copy(r, 0).start())
    pl.when(r > 0)(lambda: down_copy(r, 0).start())
    gram = jnp.zeros((3 * vecs, 5 * vecs), F32)
    for d in range(1, n):
        gram = lax.fori_loop(min((d - 1) * each, spans), min(d * each, spans), some, gram)

        @pl.when(r >= d)
        def _():
            up_copy(r - d, d - 1).wait_recv()
            pl.when(r < n - 1)(lambda: up_copy(r - d, d).start())

        @pl.when(r + d < n)
        def _():
            down_copy(r + d, d - 1).wait_recv()
            pl.when(r > 0)(lambda: down_copy(r + d, d).start())

    gram_ref[...] = jnp.zeros_like(gram_ref)
    gram_ref[:3 * vecs, :5 * vecs] = gram
    for d in range(n):
        pl.when((r >= d) & (r < n - 1))(lambda: up_copy(r - d, d).wait_send())
        pl.when((r + d < n) & (r > 0))(lambda: down_copy(r + d, d).wait_send())


def gather_pieces(x_vec, hx_vec, p_vec, hp_vec, theta, precond, n):
    vecs, length = x_vec.shape
    vmem = pl.BlockSpec(memory_space=pltpu.VMEM)
    dma = pltpu.SemaphoreType.DMA
    return pl.pallas_call(
        gather_kernel,
        out_shape=(
            jax.ShapeDtypeStruct((n, GROUPS * vecs, length // GROUPS), BF16),
            jax.ShapeDtypeStruct(x_vec.shape, F32),
            jax.ShapeDtypeStruct(SMALL, F32),
        ),
        in_specs=[vmem] * 4 + [pl.BlockSpec(memory_space=pltpu.SMEM), vmem],
        out_specs=(vmem,) * 3,
        scratch_shapes=[dma((n,)), dma((n,)), dma((n,)), dma((n,))],
        compiler_params=pltpu.CompilerParams(
            collective_id=0, has_side_effects=True, vmem_limit_bytes=VMEM_BYTES),
    )(x_vec, hx_vec, p_vec, hp_vec, theta, precond.reshape(1, length))


def block_at(shape, q, g, t, parity):
    per_group = 2 * (shape[2] // 128)
    return q * (GROUPS * per_group) + g * per_group + 2 * t + parity


def each_tile(shape, visit):
    n, tiles = shape[0], shape[2] // 128
    batch = min(tiles, 16)

    def some(i, _):
        q, t0 = i // (tiles // batch), (i % (tiles // batch)) * batch
        for t in range(batch):
            visit(q, t0 + t)
        return 0
    lax.fori_loop(0, n * tiles // batch, some, 0)


def expand(src_ref, dst_ref):
    low = row_iota() < 4
    keep = low == (lane_iota() < 64)
    shape = src_ref.shape

    def tile(q, t):
        s = src_ref[q, :, pl.ds(pl.multiple_of(t * 128, 128), 128)].astype(F32)
        for h in range(2):
            v = s[8 * h:8 * h + 8]
            vl = pltpu.roll(v, 64, 1)
            vs = pltpu.roll(v, 4, 0)
            vls = pltpu.roll(vl, 4, 0)
            g = 2 * h
            dst_ref[block_at(shape, q, g, t, 0)] = jnp.where(keep, jnp.where(low, v, vls), 0.0)
            dst_ref[block_at(shape, q, g, t, 1)] = jnp.where(keep, jnp.where(low, vl, vs), 0.0)
            dst_ref[block_at(shape, q, g + 1, t, 0)] = jnp.where(keep, jnp.where(low, vs, vl), 0.0)
            dst_ref[block_at(shape, q, g + 1, t, 1)] = jnp.where(keep, jnp.where(low, vls, v), 0.0)
    each_tile(shape, tile)


def fold(src_ref, dst_ref):
    low = row_iota() < 4
    keep = low == (lane_iota() < 64)
    shape = dst_ref.shape

    def tile(q, t):
        out = []
        for h in range(2):
            e0, o0, e1, o1 = [src_ref[block_at(shape, q, 2 * h + i // 2, t, i % 2)] for i in range(4)]
            stay = jnp.where(keep, jnp.where(low, e0, o1), pltpu.roll(jnp.where(low, o0, e1), 64, 1))
            move = jnp.where(keep, jnp.where(low, e1, o0), pltpu.roll(jnp.where(low, o1, e0), 64, 1))
            out.append(stay + pltpu.roll(move, 4, 0))
        at = pl.ds(pl.multiple_of(t * 128, 128), 128)
        dst_ref[q, :, at] = jnp.concatenate(out, 0).astype(dst_ref.dtype)
    each_tile(shape, tile)


def each_part(blocks, visit):
    def part(i, _):
        visit(pl.ds(i * PART, PART))
        return 0
    lax.fori_loop(0, blocks // PART, part, 0)


def forward_kernel(rows_ref, cols_ref, count_ref, vals_ref, own_ref, packed, fwd_ref, x_col, acc, loose):
    step, steps = pl.program_id(0), pl.num_programs(0)
    nblk = x_col.shape[0]
    quarter = lane_iota() // 32

    @pl.when(step == 0)
    def _():
        expand(own_ref, x_col)

        def clear(at):
            acc[at] = jnp.zeros((PART, 8, 128), F32)
        each_part(nblk, clear)

    count = count_ref[0]
    first = step * CHUNK
    live = jnp.clip(count - first, 0, CHUNK)

    def some_slots(i, _):
        base = i * TOGETHER
        for half in range(TOGETHER // 16):
            z0 = pl.multiple_of(base + half * 16, 16)
            for s in range(32):
                v = vals_ref[pl.ds(z0, 16), s * 128:(s + 1) * 128]
                loose[half, pl.ds(s, 16, stride=32), :] = v.astype(F32)
        for part in range(TOGETHER // 4):
            at = base + part * 4
            w = loose[part // 4, (part % 4) * 128:(part % 4 + 1) * 128, :].astype(BF16)
            packed[pl.ds(pl.multiple_of(at * 32, 128), 128), :] = w
            rows, lf = [], []
            for z in range(4):
                slot = first + at + z
                lf.append(x_col[cols_ref[slot]])
                rows.append(jnp.where(slot < count, rows_ref[slot], nblk))
            of = lax.dot_general(jnp.concatenate(lf, 0).astype(BF16), w, (((1,), (1,)), ((), ())),
                                 preferred_element_type=F32)
            for z in range(4):
                acc[rows[z]] += jnp.where(quarter == z, of[8 * z:8 * z + 8], 0.0)
        return 0
    lax.fori_loop(0, (live + TOGETHER - 1) // TOGETHER, some_slots, 0)

    @pl.when(step == steps - 1)
    def _():
        spread = spread_matrix()

        def part(at):
            x = acc[at].reshape(PART * 8, 128)
            hi = x.astype(BF16)
            lo = (x - hi.astype(F32)).astype(BF16)
            back = (((1,), (1,)), ((), ()))
            y = lax.dot_general(hi, spread, back, preferred_element_type=F32)
            y += lax.dot_general(lo, spread, back, preferred_element_type=F32)
            acc[at] = y.reshape(PART, 8, 128)
        each_part(nblk, part)
        fold(acc, fwd_ref)


def transposed_kernel(rows_ref, cols_ref, count_ref, packed, far_ref, tr_ref, x_row, acc):
    step, steps = pl.program_id(0), pl.num_programs(0)
    nblk = x_row.shape[0]
    quarter = lane_iota() // 32

    @pl.when(step == 0)
    def _():
        expand(far_ref, x_row)
        spread = spread_matrix()

        def part(at):
            x = x_row[at].reshape(PART * 8, 128).astype(BF16)
            x_row[at] = jnp.dot(x, spread, preferred_element_type=F32).reshape(PART, 8, 128)
            acc[at] = jnp.zeros((PART, 8, 128), F32)
        each_part(nblk, part)

    count = count_ref[0]
    first = step * CHUNK
    live = jnp.clip(count - first, 0, CHUNK)

    def some_slots(i, _):
        for part in range(TOGETHER // 4):
            at = i * TOGETHER + part * 4
            w = packed[pl.ds(pl.multiple_of(at * 32, 128), 128), :]
            cols, lt = [], []
            for z in range(4):
                slot = first + at + z
                lt.append(jnp.where(quarter == z, x_row[rows_ref[slot]], 0.0))
                cols.append(jnp.where(slot < count, cols_ref[slot], nblk))
            ot = jnp.dot(jnp.concatenate(lt, 0).astype(BF16), w, preferred_element_type=F32)
            for z in range(4):
                acc[cols[z]] += ot[8 * z:8 * z + 8]
        return 0
    lax.fori_loop(0, (live + TOGETHER - 1) // TOGETHER, some_slots, 0)

    pl.when(step == steps - 1)(lambda: fold(acc, tr_ref))


def cost(slots):
    return pl.CostEstimate(flops=slots * 4 * 128 * 128 * 64, bytes_accessed=slots * 16384, transcendentals=0)


def forward_products(vals, rows, cols, count, own):
    slots, size = vals.shape
    n, depth, width = own.shape
    nblk = n * GROUPS * (width // 64)
    whole = pl.BlockSpec((n, depth, width), lambda i, *_: (0, 0, 0))
    tall = CHUNK * size // 128
    return pl.pallas_call(
        forward_kernel,
        out_shape=(jax.ShapeDtypeStruct((slots * size // 128, 128), BF16), jax.ShapeDtypeStruct(own.shape, BF16)),
        grid_spec=pltpu.PrefetchScalarGridSpec(
            num_scalar_prefetch=3,
            grid=(slots // CHUNK,),
            in_specs=[pl.BlockSpec((CHUNK, size), lambda i, *_: (i, 0)), whole],
            out_specs=(pl.BlockSpec((tall, 128), lambda i, *_: (i, 0)), whole),
            scratch_shapes=[
                pltpu.VMEM((nblk, 8, 128), F32),
                pltpu.VMEM((nblk + 1, 8, 128), F32),
                pltpu.VMEM((TOGETHER // 16, 512, 128), F32),
            ],
        ),
        cost_estimate=cost(slots),
        compiler_params=pltpu.CompilerParams(vmem_limit_bytes=VMEM_BYTES),
    )(rows, cols, count, vals, own)


def transposed_products(packed, rows, cols, count, far):
    slots = rows.shape[0]
    n, depth, width = far.shape
    nblk = n * GROUPS * (width // 64)
    whole = pl.BlockSpec((n, depth, width), lambda i, *_: (0, 0, 0))
    tall = CHUNK * packed.shape[0] // slots
    return pl.pallas_call(
        transposed_kernel,
        out_shape=jax.ShapeDtypeStruct(far.shape, F32),
        grid_spec=pltpu.PrefetchScalarGridSpec(
            num_scalar_prefetch=3,
            grid=(slots // CHUNK,),
            in_specs=[pl.BlockSpec((tall, 128), lambda i, *_: (i, 0)), whole],
            out_specs=whole,
            scratch_shapes=[
                pltpu.VMEM((nblk, 8, 128), F32),
                pltpu.VMEM((nblk + 1, 8, 128), F32),
            ],
        ),
        cost_estimate=cost(slots),
        compiler_params=pltpu.CompilerParams(vmem_limit_bytes=VMEM_BYTES),
    )(rows, cols, count, packed, far)


def reduce_kernel(came_ref, tr_ref, x_ref, res_ref, p_ref, gram_ref, out_ref, sum_ref,
                  stage, landed, part, half, col_slots, row_slots,
                  send, recv, col_send, col_recv, row_send, row_recv):
    n, _, width = came_ref.shape
    vecs, length = x_ref.shape
    cols = lax.axis_size("col")
    r, c = lax.axis_index("row"), lax.axis_index("col")
    barrier = pltpu.get_barrier_semaphore()
    for d in range(1, n):
        pl.semaphore_signal(barrier, inc=1, device_id=(lax.rem(r + d, n), c), device_id_type=MESH)
    for d in range(1, cols):
        pl.semaphore_signal(barrier, inc=1, device_id=(r, lax.rem(c + d, cols)), device_id_type=MESH)

    def row_copy(d):
        return pltpu.make_async_remote_copy(
            src_ref=stage.at[d - 1], dst_ref=landed.at[d - 1],
            send_sem=send.at[d - 1], recv_sem=recv.at[d - 1],
            device_id=(lax.rem(r + d, n), c), device_id_type=MESH)

    def col_sum_copy(d):
        return pltpu.make_async_remote_copy(
            src_ref=part, dst_ref=col_slots.at[c],
            send_sem=col_send.at[d], recv_sem=col_recv.at[d],
            device_id=(r, lax.rem(c + d, cols)), device_id_type=MESH)

    def row_sum_copy(d):
        return pltpu.make_async_remote_copy(
            src_ref=half, dst_ref=row_slots.at[r],
            send_sem=row_send.at[d], recv_sem=row_recv.at[d],
            device_id=(lax.rem(r + d, n), c), device_id_type=MESH)

    def summed(d):
        q = lax.rem(r + d, n)
        return tr_ref[q] + came_ref[q].astype(F32)

    for d in range(1, n):
        stage[d - 1] = summed(d).astype(BF16)
        if d == 1:
            pl.semaphore_wait(barrier, n + cols - 2)
        row_copy(d).start()
    part[...] = gram_ref[...]
    total = summed(0)
    for d in range(1, n):
        row_copy(d).wait_recv()
        total += landed[d - 1].astype(F32)
    for g in range(GROUPS):
        out_ref[:, g * width:(g + 1) * width] = total[4 * g:4 * g + 4]

    def dots(i, sums):
        sums = list(sums)
        for t in range(8):
            at = pl.ds(pl.multiple_of((i * 8 + t) * 128, 128), 128)
            hw = out_ref[:, at]
            for v in range(3 * vecs):
                row = (x_ref, res_ref, p_ref)[v // vecs][v % vecs:v % vecs + 1, at]
                sums[v] = sums[v] + row * hw
        return tuple(sums)

    sums = lax.fori_loop(0, length // 1024, dots, tuple(jnp.zeros((vecs, 128), F32) for _ in range(3 * vecs)))
    for v in range(3 * vecs):
        part[16:16 + vecs, v:v + 1] = jnp.sum(sums[v], axis=1, keepdims=True)
    for d in range(1, cols):
        col_sum_copy(d).start()
    col_slots[c] = part[...]
    for d in range(1, cols):
        col_sum_copy(d).wait_recv()
    half[...] = jnp.sum(col_slots[...], axis=0)
    for d in range(1, n):
        row_sum_copy(d).start()
    row_slots[r] = half[...]
    for d in range(1, n):
        row_sum_copy(d).wait_recv()
    sum_ref[...] = jnp.sum(row_slots[...], axis=0) * (1.0 / (length * n * cols))

    for d in range(1, n):
        row_copy(d).wait_send()
        row_sum_copy(d).wait_send()
    for d in range(1, cols):
        col_sum_copy(d).wait_send()


def reduce_pieces(came, tr, x_vec, residue, p_vec, gram, cols):
    n, depth, width = came.shape
    vmem = pl.BlockSpec(memory_space=pltpu.VMEM)
    dma = pltpu.SemaphoreType.DMA
    return pl.pallas_call(
        reduce_kernel,
        out_shape=(jax.ShapeDtypeStruct(x_vec.shape, F32), jax.ShapeDtypeStruct(SMALL, F32)),
        in_specs=[vmem] * 6,
        out_specs=(vmem,) * 2,
        scratch_shapes=[
            pltpu.VMEM((n - 1, depth, width), BF16),
            pltpu.VMEM((n - 1, depth, width), BF16),
            pltpu.VMEM(SMALL, F32),
            pltpu.VMEM(SMALL, F32),
            pltpu.VMEM((cols,) + SMALL, F32),
            pltpu.VMEM((n,) + SMALL, F32),
            dma((n - 1,)), dma((n - 1,)),
            dma((cols,)), dma((cols,)), dma((n,)), dma((n,)),
        ],
        compiler_params=pltpu.CompilerParams(
            collective_id=1, has_side_effects=True, vmem_limit_bytes=VMEM_BYTES),
    )(came, tr, x_vec, residue, p_vec, gram)


def body(x_vec, hx_vec, p_vec, hp_vec, theta, precond, tile_vals, tile_rows, tile_cols, tile_count):
    vecs = x_vec.shape[0]
    n = lax.axis_size("row")
    cols = lax.axis_size("col")
    places = [(r, c) for r in range(n) for c in range(cols)]
    down = [(r * cols + (c + r) % cols, r * cols + c) for r, c in places]
    up = [(target, source) for source, target in down]
    rows, columns, count = tile_rows[0, 0], tile_cols[0, 0], tile_count[0]
    own, residue, gram = gather_pieces(x_vec, hx_vec, p_vec, hp_vec, theta, precond, n)
    far = lax.ppermute(own, ("row", "col"), down)
    packed, fwd = forward_products(tile_vals[0, 0], rows, columns, count, own)
    came = lax.ppermute(fwd, ("row", "col"), up)
    tr = transposed_products(packed, rows, columns, count, far)
    hw_vec, gram = reduce_pieces(came, tr, x_vec, residue, p_vec, gram, cols)
    basis = 3 * vecs
    gram_a = jnp.concatenate(
        [gram[:basis, basis:basis + vecs], gram[16:16 + vecs, :basis].T, gram[:basis, basis + vecs:basis + 2 * vecs]], 1)
    return hw_vec, gram_a, gram[:basis, :basis]


def solution(mesh):
    placed = (
        P(None, ("col", "row")),
        P(None, ("col", "row")),
        P(None, ("col", "row")),
        P(None, ("col", "row")),
        P(),
        P(("col", "row")),
        P("row", "col", None, None),
        P("row", "col", None),
        P("row", "col", None),
        P("row", "col"),
    )
    return jax.shard_map(
        body,
        mesh=mesh,
        in_specs=placed,
        out_specs=(P(None, ("col", "row")), P(), P()),
        check_vma=False,
    )
```

time: 893 us -> 98.5 us (0.11); the launches traced: 883 us -> 98.1 us
  waiting for transfers between devices: 568 us -> 0.01 us
  other arithmetic: 136 us -> 0.68 us
  Pallas kernels: 0 us -> 86.4 us
  local copies, waits for them, and re-layouts: 77.7 us -> 6.25 us
  blocking collectives: 58.5 us -> 0 us
  matrix products: 25.4 us -> 0 us
  between operations: 14.9 us -> 1.31 us
    unnamed x2 -> x0, waiting for transfers between devices: 554 us -> none
    scatter-add x2 -> x0, other arithmetic: 133 us -> none  [segment_blocks(): summed = jax.ops.segment_sum(part, index, num_segments=block_total)]
    pallas_call x0 -> x4, Pallas kernels: none -> 86.4 us  [the longest x1 31.5 us: reduce_pieces(): pl.pallas_call(reduce_kernel, out_shape=(jax.ShapeDtypeStruct(x_vec.shape...]
    psum x1 -> x0, blocking collectives: 41.1 us -> none  [body(): projected_sum = lax.psum(local_a, ('row', 'col'))]
    unnamed x17 -> x5, local copies, waits for them, and re-layouts: 35 us -> 3.24 us
    dot_general x4 -> x0, matrix products: 25.4 us -> none  [the longest x1 13.3 us: tile_terms(): jnp.einsum('zij,kzj->zki', values, picked_col, preferred_element_type=jnp...]
    another operation x3 -> x0, local copies, waits for them, and re-layouts: 24.5 us -> none  [the longest x1 23.9 us: body(): values = tile_vals[0, 0].reshape(slot_total, BLOCK, BLOCK)]
    all_gather x1 -> x0, blocking collectives: 17.4 us -> none  [body(): own_segment = lax.all_gather(w_send, 'row', axis=1, tiled=True)]
  transfers between devices with their start and end apart: 5 -> 2, of which waited for: 2 -> 0; matrix products, arithmetic and copies ran while one was open for 24% -> 0% of each run, Pallas kernels for 0% -> 38%
where the time goes in v4:
time: 98.5 us; the launch traced here: 98.1 us
  Pallas kernels  86.4 us (88%)
  local copies, waits for them, and re-layouts  6.25 us (6%)
  starting transfers between devices  3.39 us (3%)
  between operations  1.31 us (1%)
    pallas_call x1, Pallas kernels, reduce_pieces(): pl.pallas_call(reduce_kernel, out_shape=(jax.ShapeDtypeStruct(x_vec.shape...  31.5 us
    pallas_call x1, Pallas kernels, forward_products(): pl.pallas_call(forward_kernel, out_shape=(jax.ShapeDtypeStruct((slots * s...  21.8 us
    pallas_call x1, Pallas kernels, gather_pieces(): pl.pallas_call(gather_kernel, out_shape=(jax.ShapeDtypeStruct((n, GROUPS...  18 us
    pallas_call x1, Pallas kernels, transposed_products(): pl.pallas_call(transposed_kernel, out_shape=jax.ShapeDtypeStruct(far.shap...  15.1 us
    unnamed x5, local copies, waits for them, and re-layouts  3.24 us
  transfers between devices with their start and end apart: 2, of which 0 were waited for; matrix products, arithmetic and copies ran while one was open for 0% of the time, Pallas kernels for 38%

profile of v4, /device:TPU:0, one launch (start us, length us, event | category | flops | bytes accessed | tf_op | source)
XLA Modules:
  0.0 98.1 jit_solution(14378789887556175560)
XLA Ops:
  0.6 18.0 %shard_map.121 = (bf16[4,16,4096]{2,1,0:T(8,128)(2,1)}, f32[4,16384]{1,0:T(4,128)}, f32[24,128]{1,0:T(8,128)}) custom-call(f32[4,16384]{1,0:T(4,128)} %x_ref.3, f32[4,16384]{1,0:T(4,128)} %hx_ref.1, f32[4,16384]{1,0:T(4,128)} %p_ref.3, f32[4,16384]{1,0:T(4,128)} %hp_ref.1, f32[4]{0:T(128)} %theta_ref.1, f32[1,16384]{1,0:T(1,128)} %bitcast.9), custom_call_target="tpu_custom_call" | custom-call | tf_op jit(solution)/shard_map/pallas_call | solution.py:110
  18.7 1.7 %collective-permute-start.1 = (bf16[4,16,4096]{2,1,0:T(8,128)(2,1)}, bf16[4,16,4096]{2,1,0:T(8,128)(2,1)S(1)}, u32[]{:S(2)}, u32[]{:S(2)}) collective-permute-start(bf16[4,16,4096]{2,1,0:T(8,128)(2,1)} %get-tuple-element.10.own_ref), channel_id=1, source_target_pairs={{0,0},{1,1},{2,2},{3,3},{4,4},{5,5},{6,6},{7,7},{9,8},{10,9},{11,1... | collective-permute-start | bytes 1572872 | tf_op jit(solution)/shard_map/ppermute | solution.py:447
  21.0 21.8 %shard_map.122 = (bf16[32768,128]{1,0:T(8,128)(2,1)}, bf16[4,16,4096]{2,1,0:T(8,128)(2,1)}) custom-call(s32[1024]{0:T(1024)} %bitcast.11, s32[1024]{0:T(1024)} %bitcast.13, s32[1]{0:T(128)} %bitcast.7.count_ref, bf16[1024,4096]{1,0:T(8,128)(2,1)} %bitcast.10, bf16[4,16,4096]{2,1,0:T(8,128)(2,1)} %get-tuple-element.10.own_ref), custom_call_target="tpu_custom_call" | custom-call | flops 4294967296 | bytes 16777216 | tf_op jit(solution)/shard_map/pallas_call | solution.py:290
  42.8 1.7 %collective-permute-start = (bf16[4,16,4096]{2,1,0:T(8,128)(2,1)}, bf16[4,16,4096]{2,1,0:T(8,128)(2,1)S(1)}, u32[]{:S(2)}, u32[]{:S(2)}) collective-permute-start(bf16[4,16,4096]{2,1,0:T(8,128)(2,1)} %get-tuple-element.11), channel_id=1, source_target_pairs={{0,0},{1,1},{2,2},{3,3},{4,4},{5,5},{6,6},{7,7},{8,9},{9,10},{10,1... | collective-permute-start | bytes 1572872 | tf_op jit(solution)/shard_map/ppermute | solution.py:449
  44.5 0.0 collective-permute-done.1.far_ref
  44.5 0.0 copy-start.1
  44.5 0.8 copy-done.1
  45.3 15.1 %shard_map.123.tr_ref = f32[4,16,4096]{2,1,0:T(8,128)} custom-call(s32[1024]{0:T(1024)} %bitcast.12, s32[1024]{0:T(1024)} %bitcast.14, s32[1]{0:T(128)} %bitcast.8.count_ref, bf16[32768,128]{1,0:T(8,128)(2,1)} %get-tuple-element.12.packed, bf16[4,16,4096]{2,1,0:T(8,128)(2,1)} %copy-done.1), custom_call_target="tpu_custom_call" | custom-call | flops 4294967296 | bytes 16777216 | tf_op jit(solution)/shard_map/pallas_call | solution.py:315
  60.4 0.0 collective-permute-done.came_ref
  60.4 0.0 copy-start
  60.4 0.8 copy-done
  61.2 31.5 %shard_map.124 = (f32[4,16384]{1,0:T(4,128)}, f32[24,128]{1,0:T(8,128)}) custom-call(bf16[4,16,4096]{2,1,0:T(8,128)(2,1)} %copy-done, f32[4,16,4096]{2,1,0:T(8,128)} %shard_map.123.tr_ref, f32[4,16384]{1,0:T(4,128)} %x_ref.3, f32[4,16384]{1,0:T(4,128)} %get-tuple-element.13.res_ref, f32[4,16384]{1,0:T(4,128)} %p_ref.3, f32[24,128]{1,0:T(8,128)} %get-tuple-element.14.gram_ref), custom_call_target="tpu_custom_call" | custom-call | tf_op jit(solution)/shard_map/pallas_call | solution.py:418
  92.7 1.3 %slice.15 = f32[12,12]{1,0:T(8,128)} slice(f32[24,128]{1,0:T(8,128)} %get-tuple-element.16), slice={[0:12], [0:12]} | slice | bytes 1152 | tf_op jit(solution)/shard_map/slice | solution.py:455
  94.0 0.8 fusion
  94.8 0.8 copy.13
  95.7 0.1 slice_bitcast_fusion
  95.7 0.7 pad_maximum_fusion
  96.4 1.7 %copy.16 = f32[4,16384]{1,0:T(4,128)} copy(f32[4,16384]{1,0:T(4,128)} %get-tuple-element.22) | data formatting | bytes 524288
Async XLA Ops:
  18.7 25.8 %collective-permute-start.1 = (bf16[4,16,4096]{2,1,0:T(8,128)(2,1)}, bf16[4,16,4096]{2,1,0:T(8,128)(2,1)S(1)}, u32[]{:S(2)}, u32[]{:S(2)}) collective-permute-start(bf16[4,16,4096]{2,1,0:T(8,128)(2,1)} %get-tuple-element.10.own_ref), channel_id=1, source_target_pairs={{0,0},{1,1},{2,2},{3,3},{4,4},{5,5},{6,6},{7,7},{9,8},{10,9},{11,1... | collective-permute-start | bytes 1572872 | tf_op jit(solution)/shard_map/ppermute | solution.py:447
  42.8 17.6 %collective-permute-start = (bf16[4,16,4096]{2,1,0:T(8,128)(2,1)}, bf16[4,16,4096]{2,1,0:T(8,128)(2,1)S(1)}, u32[]{:S(2)}, u32[]{:S(2)}) collective-permute-start(bf16[4,16,4096]{2,1,0:T(8,128)(2,1)} %get-tuple-element.11), channel_id=1, source_target_pairs={{0,0},{1,1},{2,2},{3,3},{4,4},{5,5},{6,6},{7,7},{8,9},{9,10},{10,1... | collective-permute-start | bytes 1572872 | tf_op jit(solution)/shard_map/ppermute | solution.py:449
  44.5 0.8 copy-start.1
  60.4 0.8 copy-start

commit v5 on v4

--- a/solution.py
+++ b/solution.py
@@ -10,7 +10,7 @@
 GROUPS = 4
 CHUNK = 128
 TOGETHER = 32
-PART = 64
+PART = 128
 SMALL = (24, 128)
 MESH = pl.DeviceIdType.MESH
 F32 = jnp.float32
@@ -32,10 +32,10 @@
     return jnp.where((a % 64) == 2 * (b % 32) + a // 64, 1.0, 0.0).astype(BF16)
 
 
-def gather_kernel(x_ref, hx_ref, p_ref, hp_ref, theta_ref, precond_ref, own_ref, res_ref, gram_ref,
+def gather_kernel(x_ref, hx_ref, theta_ref, precond_ref, own_ref, res_ref,
                   up_send, up_recv, down_send, down_recv):
     n, _, width = own_ref.shape
-    vecs, length = x_ref.shape
+    vecs = x_ref.shape[0]
     r, c = lax.axis_index("row"), lax.axis_index("col")
     barrier = pltpu.get_barrier_semaphore()
 
@@ -67,25 +67,9 @@
             send_sem=down_send.at[d], recv_sem=down_recv.at[d],
             device_id=(r - 1, c), device_id_type=MESH)
 
-    span = min(length, 2048)
-    spans = length // span
-    each = -(-spans // (n - 1))
-    left = [x_ref, res_ref, p_ref]
-    right = left + [hx_ref, hp_ref]
-
-    def some(i, total):
-        at = pl.ds(pl.multiple_of(i * span, span), span)
-        v = jnp.concatenate([ref[:, at] for ref in left], 0)
-        w = jnp.concatenate([ref[:, at] for ref in right], 0)
-        return total + lax.dot_general(v, w, (((1,), (1,)), ((), ())), precision=lax.Precision.HIGHEST,
-                                       preferred_element_type=F32)
-
     pl.when(r < n - 1)(lambda: up_copy(r, 0).start())
     pl.when(r > 0)(lambda: down_copy(r, 0).start())
-    gram = jnp.zeros((3 * vecs, 5 * vecs), F32)
-    for d in range(1, n):
-        gram = lax.fori_loop(min((d - 1) * each, spans), min(d * each, spans), some, gram)
-
+    for d in range(1, n):
         @pl.when(r >= d)
         def _():
             up_copy(r - d, d - 1).wait_recv()
@@ -96,14 +80,12 @@
             down_copy(r + d, d - 1).wait_recv()
             pl.when(r > 0)(lambda: down_copy(r + d, d).start())
 
-    gram_ref[...] = jnp.zeros_like(gram_ref)
-    gram_ref[:3 * vecs, :5 * vecs] = gram
     for d in range(n):
         pl.when((r >= d) & (r < n - 1))(lambda: up_copy(r - d, d).wait_send())
         pl.when((r + d < n) & (r > 0))(lambda: down_copy(r + d, d).wait_send())
 
 
-def gather_pieces(x_vec, hx_vec, p_vec, hp_vec, theta, precond, n):
+def gather_pieces(x_vec, hx_vec, theta, precond, n):
     vecs, length = x_vec.shape
     vmem = pl.BlockSpec(memory_space=pltpu.VMEM)
     dma = pltpu.SemaphoreType.DMA
@@ -112,14 +94,13 @@
         out_shape=(
             jax.ShapeDtypeStruct((n, GROUPS * vecs, length // GROUPS), BF16),
             jax.ShapeDtypeStruct(x_vec.shape, F32),
-            jax.ShapeDtypeStruct(SMALL, F32),
         ),
-        in_specs=[vmem] * 4 + [pl.BlockSpec(memory_space=pltpu.SMEM), vmem],
-        out_specs=(vmem,) * 3,
+        in_specs=[vmem] * 2 + [pl.BlockSpec(memory_space=pltpu.SMEM), vmem],
+        out_specs=(vmem,) * 2,
         scratch_shapes=[dma((n,)), dma((n,)), dma((n,)), dma((n,))],
         compiler_params=pltpu.CompilerParams(
             collective_id=0, has_side_effects=True, vmem_limit_bytes=VMEM_BYTES),
-    )(x_vec, hx_vec, p_vec, hp_vec, theta, precond.reshape(1, length))
+    )(x_vec, hx_vec, theta, precond.reshape(1, length))
 
 
 def block_at(shape, q, g, t, parity):
@@ -129,7 +110,7 @@
 
 def each_tile(shape, visit):
     n, tiles = shape[0], shape[2] // 128
-    batch = min(tiles, 16)
+    batch = min(tiles, 32)
 
     def some(i, _):
         q, t0 = i // (tiles // batch), (i % (tiles // batch)) * batch
@@ -330,7 +311,7 @@
     )(rows, cols, count, packed, far)
 
 
-def reduce_kernel(came_ref, tr_ref, x_ref, res_ref, p_ref, gram_ref, out_ref, sum_ref,
+def reduce_kernel(came_ref, tr_ref, x_ref, res_ref, p_ref, hx_ref, hp_ref, out_ref, sum_ref,
                   stage, landed, part, half, col_slots, row_slots,
                   send, recv, col_send, col_recv, row_send, row_recv):
     n, _, width = came_ref.shape
@@ -370,7 +351,19 @@
         if d == 1:
             pl.semaphore_wait(barrier, n + cols - 2)
         row_copy(d).start()
-    part[...] = gram_ref[...]
+    span = min(length, 2048)
+    left = [x_ref, res_ref, p_ref]
+    right = left + [hx_ref, hp_ref]
+
+    def early(i, gram):
+        at = pl.ds(pl.multiple_of(i * span, span), span)
+        v = jnp.concatenate([ref[:, at] for ref in left], 0)
+        w = jnp.concatenate([ref[:, at] for ref in right], 0)
+        return gram + lax.dot_general(v, w, (((1,), (1,)), ((), ())), precision=lax.Precision.HIGHEST,
+                                      preferred_element_type=F32)
+
+    part[...] = jnp.zeros_like(part)
+    part[:3 * vecs, :5 * vecs] = lax.fori_loop(0, length // span, early, jnp.zeros((3 * vecs, 5 * vecs), F32))
     total = summed(0)
     for d in range(1, n):
         row_copy(d).wait_recv()
@@ -411,14 +404,14 @@
         col_sum_copy(d).wait_send()
 
 
-def reduce_pieces(came, tr, x_vec, residue, p_vec, gram, cols):
+def reduce_pieces(came, tr, x_vec, residue, p_vec, hx_vec, hp_vec, cols):
     n, depth, width = came.shape
     vmem = pl.BlockSpec(memory_space=pltpu.VMEM)
     dma = pltpu.SemaphoreType.DMA
     return pl.pallas_call(
         reduce_kernel,
         out_shape=(jax.ShapeDtypeStruct(x_vec.shape, F32), jax.ShapeDtypeStruct(SMALL, F32)),
-        in_specs=[vmem] * 6,
+        in_specs=[vmem] * 7,
         out_specs=(vmem,) * 2,
         scratch_shapes=[
             pltpu.VMEM((n - 1, depth, width), BF16),
@@ -432,27 +425,47 @@
         ],
         compiler_params=pltpu.CompilerParams(
             collective_id=1, has_side_effects=True, vmem_limit_bytes=VMEM_BYTES),
-    )(came, tr, x_vec, residue, p_vec, gram)
+    )(came, tr, x_vec, residue, p_vec, hx_vec, hp_vec)
+
+
+def finish_kernel(hw_ref, sum_ref, out_ref, a_ref, b_ref):
+    out_ref[...] = hw_ref[...]
+    vecs = hw_ref.shape[0]
+    basis = 3 * vecs
+    gram = sum_ref[...]
+    b_ref[...] = gram[:basis, :basis]
+    a_ref[:, :vecs] = gram[:basis, basis:basis + vecs]
+    turned = jnp.transpose(gram[16:24])
+    a_ref[:, vecs:2 * vecs] = turned[:basis, :vecs]
+    a_ref[:, 2 * vecs:] = gram[:basis, basis + vecs:basis + 2 * vecs]
+
+
+def finish(hw_vec, gram):
+    basis = 3 * hw_vec.shape[0]
+    vmem = pl.BlockSpec(memory_space=pltpu.VMEM)
+    square = jax.ShapeDtypeStruct((basis, basis), F32)
+    return pl.pallas_call(
+        finish_kernel,
+        out_shape=(jax.ShapeDtypeStruct(hw_vec.shape, F32), square, square),
+        in_specs=[vmem] * 2,
+        out_specs=(vmem,) * 3,
+    )(hw_vec, gram)
 
 
 def body(x_vec, hx_vec, p_vec, hp_vec, theta, precond, tile_vals, tile_rows, tile_cols, tile_count):
-    vecs = x_vec.shape[0]
     n = lax.axis_size("row")
     cols = lax.axis_size("col")
     places = [(r, c) for r in range(n) for c in range(cols)]
     down = [(r * cols + (c + r) % cols, r * cols + c) for r, c in places]
     up = [(target, source) for source, target in down]
     rows, columns, count = tile_rows[0, 0], tile_cols[0, 0], tile_count[0]
-    own, residue, gram = gather_pieces(x_vec, hx_vec, p_vec, hp_vec, theta, precond, n)
+    own, residue = gather_pieces(x_vec, hx_vec, theta, precond, n)
     far = lax.ppermute(own, ("row", "col"), down)
     packed, fwd = forward_products(tile_vals[0, 0], rows, columns, count, own)
     came = lax.ppermute(fwd, ("row", "col"), up)
     tr = transposed_products(packed, rows, columns, count, far)
-    hw_vec, gram = reduce_pieces(came, tr, x_vec, residue, p_vec, gram, cols)
-    basis = 3 * vecs
-    gram_a = jnp.concatenate(
-        [gram[:basis, basis:basis + vecs], gram[16:16 + vecs, :basis].T, gram[:basis, basis + vecs:basis + 2 * vecs]], 1)
-    return hw_vec, gram_a, gram[:basis, :basis]
+    hw_vec, gram = reduce_pieces(came, tr, x_vec, residue, p_vec, hx_vec, hp_vec, cols)
+    return finish(hw_vec, gram)
 
 
 def solution(mesh):

time: 98.5 us -> 91.3 us (0.927)
  local copies, waits for them, and re-layouts: 6.25 us -> 1.58 us
  Pallas kernels: 86.4 us -> 84.9 us
    pallas_call x1, Pallas kernels: 31.5 us -> 25.3 us  [reduce_pieces(): pl.pallas_call(reduce_kernel, out_shape=(jax.ShapeDtypeStruct(x_vec.shape...]
    pallas_call x1, Pallas kernels: 21.8 us -> 24.7 us  [forward_products(): pl.pallas_call(forward_kernel, out_shape=(jax.ShapeDtypeStruct((slots * s...]
    slice x2 -> x0, local copies, waits for them, and re-layouts: 2.14 us -> none  [the longest x1 1.3 us: body(): return (hw_vec, gram_a, gram[:basis, :basis])]
    pallas_call x0 -> x1, Pallas kernels: none -> 1.73 us  [finish(): pl.pallas_call(finish_kernel, out_shape=(jax.ShapeDtypeStruct(hw_vec.shap...]
    unnamed x5 -> x4, local copies, waits for them, and re-layouts: 3.24 us -> 1.58 us
  transfers between devices with their start and end apart: 2 -> 2, of which waited for: 0 -> 0; matrix products, arithmetic and copies ran while one was open for 0% -> 0% of each run, Pallas kernels for 38% -> 44%
where the time goes in v5:
time: 91.3 us; the launch traced here: 91.2 us
  Pallas kernels  84.9 us (93%)
  starting transfers between devices  3.39 us (4%)
  local copies, waits for them, and re-layouts  1.58 us (2%)
  between operations  1.3 us (1%)
    pallas_call x1, Pallas kernels, reduce_pieces(): pl.pallas_call(reduce_kernel, out_shape=(jax.ShapeDtypeStruct(x_vec.shape...  25.3 us
    pallas_call x1, Pallas kernels, forward_products(): pl.pallas_call(forward_kernel, out_shape=(jax.ShapeDtypeStruct((slots * s...  24.7 us
    pallas_call x1, Pallas kernels, gather_pieces(): pl.pallas_call(gather_kernel, out_shape=(jax.ShapeDtypeStruct((n, GROUPS...  17.8 us
    pallas_call x1, Pallas kernels, transposed_products(): pl.pallas_call(transposed_kernel, out_shape=jax.ShapeDtypeStruct(far.shap...  15.3 us
  transfers between devices with their start and end apart: 2, of which 0 were waited for; matrix products, arithmetic and copies ran while one was open for 0% of the time, Pallas kernels for 44%

profile of v5, /device:TPU:0, one launch (start us, length us, event | category | flops | bytes accessed | tf_op | source)
XLA Modules:
  0.0 91.2 jit_solution(12020125216104939912)
XLA Ops:
  0.6 17.8 %shard_map.121 = (bf16[4,16,4096]{2,1,0:T(8,128)(2,1)}, f32[4,16384]{1,0:T(4,128)}) custom-call(f32[4,16384]{1,0:T(4,128)} %x_ref.3, f32[4,16384]{1,0:T(4,128)} %hx_ref.3, f32[4]{0:T(128)} %theta_ref.1, f32[1,16384]{1,0:T(1,128)} %bitcast.7), custom_call_target="tpu_custom_call" | custom-call | tf_op jit(solution)/shard_map/pallas_call | solution.py:92
  18.5 1.7 %collective-permute-start.1 = (bf16[4,16,4096]{2,1,0:T(8,128)(2,1)}, bf16[4,16,4096]{2,1,0:T(8,128)(2,1)S(1)}, u32[]{:S(2)}, u32[]{:S(2)}) collective-permute-start(bf16[4,16,4096]{2,1,0:T(8,128)(2,1)} %get-tuple-element.9.own_ref), channel_id=1, source_target_pairs={{0,0},{1,1},{2,2},{3,3},{4,4},{5,5},{6,6},{7,7},{9,8},{10,9},{11,1... | collective-permute-start | bytes 1572872 | tf_op jit(solution)/shard_map/ppermute | solution.py:463
  20.8 24.7 %shard_map.122 = (bf16[32768,128]{1,0:T(8,128)(2,1)}, bf16[4,16,4096]{2,1,0:T(8,128)(2,1)}) custom-call(s32[1024]{0:T(1024)} %bitcast.9, s32[1024]{0:T(1024)} %bitcast.11, s32[1]{0:T(128)} %bitcast.5.count_ref, bf16[1024,4096]{1,0:T(8,128)(2,1)} %bitcast.8, bf16[4,16,4096]{2,1,0:T(8,128)(2,1)} %get-tuple-element.9.own_ref), custom_call_target="tpu_custom_call" | custom-call | flops 4294967296 | bytes 16777216 | tf_op jit(solution)/shard_map/pallas_call | solution.py:271
  45.5 1.7 %collective-permute-start = (bf16[4,16,4096]{2,1,0:T(8,128)(2,1)}, bf16[4,16,4096]{2,1,0:T(8,128)(2,1)S(1)}, u32[]{:S(2)}, u32[]{:S(2)}) collective-permute-start(bf16[4,16,4096]{2,1,0:T(8,128)(2,1)} %get-tuple-element.10), channel_id=1, source_target_pairs={{0,0},{1,1},{2,2},{3,3},{4,4},{5,5},{6,6},{7,7},{8,9},{9,10},{10,1... | collective-permute-start | bytes 1572872 | tf_op jit(solution)/shard_map/ppermute | solution.py:465
  47.2 0.0 collective-permute-done.1.far_ref
  47.2 0.0 copy-start.1
  47.2 0.8 copy-done.1
  48.0 15.3 %shard_map.123.tr_ref = f32[4,16,4096]{2,1,0:T(8,128)} custom-call(s32[1024]{0:T(1024)} %bitcast.10, s32[1024]{0:T(1024)} %bitcast.12, s32[1]{0:T(128)} %bitcast.6.count_ref, bf16[32768,128]{1,0:T(8,128)(2,1)} %get-tuple-element.11.packed, bf16[4,16,4096]{2,1,0:T(8,128)(2,1)} %copy-done.1), custom_call_target="tpu_custom_call" | custom-call | flops 4294967296 | bytes 16777216 | tf_op jit(solution)/shard_map/pallas_call | solution.py:296
  63.3 0.0 collective-permute-done.came_ref
  63.3 0.0 copy-start
  63.3 0.8 copy-done
  64.1 25.3 %shard_map.124 = (f32[4,16384]{1,0:T(4,128)}, f32[24,128]{1,0:T(8,128)}) custom-call(bf16[4,16,4096]{2,1,0:T(8,128)(2,1)} %copy-done, f32[4,16,4096]{2,1,0:T(8,128)} %shard_map.123.tr_ref, f32[4,16384]{1,0:T(4,128)} %x_ref.3, f32[4,16384]{1,0:T(4,128)} %get-tuple-element.12.res_ref, f32[4,16384]{1,0:T(4,128)} %p_ref.1, f32[4,16384]{1,0:T(4,128)} %hx_ref.3, ...), custom_call_target="tpu_custom_call" | custom-call | tf_op jit(solution)/shard_map/pallas_call | solution.py:411
  89.4 1.7 %shard_map.125 = (f32[4,16384]{1,0:T(4,128)}, f32[12,12]{1,0:T(8,128)}, f32[12,12]{1,0:T(8,128)}) custom-call(f32[4,16384]{1,0:T(4,128)} %get-tuple-element.13.hw_ref, f32[24,128]{1,0:T(8,128)} %get-tuple-element.14.sum_ref), custom_call_target="tpu_custom_call" | custom-call | tf_op jit(solution)/shard_map/pallas_call | solution.py:447
Async XLA Ops:
  18.5 28.7 %collective-permute-start.1 = (bf16[4,16,4096]{2,1,0:T(8,128)(2,1)}, bf16[4,16,4096]{2,1,0:T(8,128)(2,1)S(1)}, u32[]{:S(2)}, u32[]{:S(2)}) collective-permute-start(bf16[4,16,4096]{2,1,0:T(8,128)(2,1)} %get-tuple-element.9.own_ref), channel_id=1, source_target_pairs={{0,0},{1,1},{2,2},{3,3},{4,4},{5,5},{6,6},{7,7},{9,8},{10,9},{11,1... | collective-permute-start | bytes 1572872 | tf_op jit(solution)/shard_map/ppermute | solution.py:463
  45.5 17.8 %collective-permute-start = (bf16[4,16,4096]{2,1,0:T(8,128)(2,1)}, bf16[4,16,4096]{2,1,0:T(8,128)(2,1)S(1)}, u32[]{:S(2)}, u32[]{:S(2)}) collective-permute-start(bf16[4,16,4096]{2,1,0:T(8,128)(2,1)} %get-tuple-element.10), channel_id=1, source_target_pairs={{0,0},{1,1},{2,2},{3,3},{4,4},{5,5},{6,6},{7,7},{8,9},{9,10},{10,1... | collective-permute-start | bytes 1572872 | tf_op jit(solution)/shard_map/ppermute | solution.py:465
  47.2 0.8 copy-start.1
  63.3 0.8 copy-start

commit v6 on v5

--- a/solution.py
+++ b/solution.py
@@ -8,14 +8,14 @@
 
 BLOCK = 64
 GROUPS = 4
-CHUNK = 128
+CHUNK = 256
 TOGETHER = 32
 PART = 128
 SMALL = (24, 128)
 MESH = pl.DeviceIdType.MESH
 F32 = jnp.float32
 BF16 = jnp.bfloat16
-VMEM_BYTES = 58 * 1024 * 1024
+VMEM_BYTES = 32 * 1024 * 1024
 
 
 def row_iota():

time: 91.3 us -> 88.5 us (0.969)
  Pallas kernels: 84.9 us -> 75.8 us
  local copies, waits for them, and re-layouts: 1.58 us -> 9.44 us
  starting transfers between devices: 3.39 us -> 1.52 us
    pallas_call x1, Pallas kernels: 25.3 us -> 40.5 us  [reduce_pieces(): pl.pallas_call(reduce_kernel, out_shape=(jax.ShapeDtypeStruct(x_vec.shape...]
    pallas_call x1, Pallas kernels: 24.7 us -> 10.4 us  [forward_products(): pl.pallas_call(forward_kernel, out_shape=(jax.ShapeDtypeStruct((slots * s...]
    pallas_call x1, Pallas kernels: 15.3 us -> 6.69 us  [transposed_products(): pl.pallas_call(transposed_kernel, out_shape=jax.ShapeDtypeStruct(far.shap...]
    unnamed x4 -> x26, local copies, waits for them, and re-layouts: 1.58 us -> 9.44 us
    pallas_call x1, Pallas kernels: 17.8 us -> 16.4 us  [gather_pieces(): pl.pallas_call(gather_kernel, out_shape=(jax.ShapeDtypeStruct((n, GROUPS...]
    ppermute x1, starting transfers between devices: 1.7 us -> 0.69 us  [body(): far = lax.ppermute(own, ('row', 'col'), down)]
  transfers between devices with their start and end apart: 2 -> 2, of which waited for: 0 -> 0; matrix products, arithmetic and copies ran while one was open for 0% -> 0% of each run, Pallas kernels for 44% -> 19%
where the time goes in v6:
time: 88.5 us; the launch traced here: 88.2 us
  Pallas kernels  75.8 us (86%)
  local copies, waits for them, and re-layouts  9.44 us (11%)
  starting transfers between devices  1.52 us (2%)
  between operations  1.44 us (2%)
    pallas_call x1, Pallas kernels, reduce_pieces(): pl.pallas_call(reduce_kernel, out_shape=(jax.ShapeDtypeStruct(x_vec.shape...  40.5 us
    pallas_call x1, Pallas kernels, gather_pieces(): pl.pallas_call(gather_kernel, out_shape=(jax.ShapeDtypeStruct((n, GROUPS...  16.4 us
    pallas_call x1, Pallas kernels, forward_products(): pl.pallas_call(forward_kernel, out_shape=(jax.ShapeDtypeStruct((slots * s...  10.4 us
    unnamed x26, local copies, waits for them, and re-layouts  9.44 us
    pallas_call x1, Pallas kernels, transposed_products(): pl.pallas_call(transposed_kernel, out_shape=jax.ShapeDtypeStruct(far.shap...  6.69 us
  transfers between devices with their start and end apart: 2, of which 0 were waited for; matrix products, arithmetic and copies ran while one was open for 0% of the time, Pallas kernels for 19%

profile of v6, /device:TPU:0, one launch (start us, length us, event | category | flops | bytes accessed | tf_op | source)
XLA Modules:
  0.0 88.2 jit_solution(12530610749190861734)
XLA Ops:
  0.6 0.0 copy-start
  0.6 0.9 %copy-done = f32[4,16384]{1,0:T(4,128)S(1)} copy-done((f32[4,16384]{1,0:T(4,128)S(1)}, f32[4,16384]{1,0:T(4,128)}, u32[]{:S(2)}) %copy-start) | copy-done | bytes 262168
  1.6 0.0 copy-start.2
  1.6 0.9 %copy-done.2 = f32[4,16384]{1,0:T(4,128)S(1)} copy-done((f32[4,16384]{1,0:T(4,128)S(1)}, f32[4,16384]{1,0:T(4,128)}, u32[]{:S(2)}) %copy-start.2) | copy-done | bytes 262168
  2.5 0.0 copy-start.7
  2.5 0.8 copy-done.7
  3.4 0.0 copy-start.9
  3.4 0.7 copy-done.9
  4.0 16.4 %shard_map.121 = (bf16[4,16,4096]{2,1,0:T(8,128)(2,1)S(1)}, f32[4,16384]{1,0:T(4,128)S(1)}) custom-call(f32[4,16384]{1,0:T(4,128)S(1)} %copy-done, f32[4,16384]{1,0:T(4,128)S(1)} %copy-done.2, f32[4]{0:T(128)S(1)} %copy-done.9, f32[1,16384]{1,0:T(1,128)S(1)} %bitcast.7), custom_call_target="tpu_custom_call" | custom-call | tf_op jit(solution)/shard_map/pallas_call | solution.py:92
  20.5 0.7 collective-permute-start.1
  21.8 0.0 copy-start.10
  21.8 3.4 %copy-done.10 = bf16[1,1,1024,4096]{3,2,1,0:T(8,128)(2,1)S(1)} copy-done((bf16[1,1,1024,4096]{3,2,1,0:T(8,128)(2,1)S(1)}, bf16[1,1,1024,4096]{3,2,1,0:T(8,128)(2,1)}, u32[]{:S(2)}) %copy-start.10) | copy-done | bytes 8388632
  25.2 0.0 copy-start.11
  25.2 0.7 copy-done.11
  25.9 0.0 copy-start.12
  25.9 0.7 copy-done.12
  26.6 10.4 %shard_map.122 = (bf16[32768,128]{1,0:T(8,128)(2,1)S(1)}, bf16[4,16,4096]{2,1,0:T(8,128)(2,1)S(1)}) custom-call(s32[1024]{0:T(1024)S(1)} %bitcast.9, s32[1024]{0:T(1024)S(1)} %bitcast.11, s32[1]{0:T(128)} %bitcast.5.count_ref, bf16[1024,4096]{1,0:T(8,128)(2,1)S(1)} %bitcast.8, bf16[4,16,4096]{2,1,0:T(8,128)(2,1)S(1)} %get-tuple-element.9.own_ref), custom_call_target="tpu_custom_call" | custom-call | flops 4294967296 | bytes 16777216 | tf_op jit(solution)/shard_map/pallas_call | solution.py:271
  37.0 0.0 copy-start.1
  37.0 0.0 copy-start.3
  37.1 0.0 copy-start.5
  37.1 0.0 copy-start.6
  37.1 0.8 collective-permute-start
  37.9 0.0 collective-permute-done.1.far_ref
  37.9 6.7 %shard_map.123.tr_ref = f32[4,16,4096]{2,1,0:T(8,128)S(1)} custom-call(s32[1024]{0:T(1024)S(1)} %bitcast.10, s32[1024]{0:T(1024)S(1)} %bitcast.12, s32[1]{0:T(128)} %bitcast.6.count_ref, bf16[32768,128]{1,0:T(8,128)(2,1)S(1)} %get-tuple-element.11.packed, bf16[4,16,4096]{2,1,0:T(8,128)(2,1)S(1)} %collective-permute-done.1.far_ref), custom_call_target="tpu_custom_call" | custom-call | flops 4294967296 | bytes 16777216 | tf_op jit(solution)/shard_map/pallas_call | solution.py:296
  44.6 0.0 collective-permute-done.came_ref
  44.6 0.0 copy-done.1
  44.6 0.0 copy-done.3
  44.7 0.0 copy-done.5
  44.7 0.0 copy-done.6
  44.7 40.5 %shard_map.124 = (f32[4,16384]{1,0:T(4,128)S(1)}, f32[24,128]{1,0:T(8,128)S(1)}) custom-call(bf16[4,16,4096]{2,1,0:T(8,128)(2,1)S(1)} %collective-permute-done.came_ref, f32[4,16,4096]{2,1,0:T(8,128)S(1)} %shard_map.123.tr_ref, f32[4,16384]{1,0:T(4,128)S(1)} %copy-done.1, f32[4,16384]{1,0:T(4,128)S(1)} %get-tuple-element.12.res_ref, ...), custom_call_target="tpu_custom_call" | custom-call | tf_op jit(solution)/shard_map/pallas_call | solution.py:411
  85.1 0.0 copy-start.4
  85.2 0.7 copy-done.4
  85.8 0.0 copy-start.8
  85.8 0.6 copy-done.8
  86.4 1.7 %shard_map.125 = (f32[4,16384]{1,0:T(4,128)}, f32[12,12]{1,0:T(8,128)}, f32[12,12]{1,0:T(8,128)}) custom-call(f32[4,16384]{1,0:T(4,128)} %copy-done.4, f32[24,128]{1,0:T(8,128)} %copy-done.8), custom_call_target="tpu_custom_call" | custom-call | tf_op jit(solution)/shard_map/pallas_call | solution.py:447
Async XLA Ops:
  0.6 1.0 %copy-start = (f32[4,16384]{1,0:T(4,128)S(1)}, f32[4,16384]{1,0:T(4,128)}, u32[]{:S(2)}) copy-start(f32[4,16384]{1,0:T(4,128)} %x_ref.3) | copy-start | bytes 786436
  1.6 0.9 %copy-start.2 = (f32[4,16384]{1,0:T(4,128)S(1)}, f32[4,16384]{1,0:T(4,128)}, u32[]{:S(2)}) copy-start(f32[4,16384]{1,0:T(4,128)} %hx_ref.3) | copy-start | bytes 786436
  2.5 0.8 copy-start.7
  3.4 0.7 copy-start.9
  20.5 17.5 %collective-permute-start.1 = (bf16[4,16,4096]{2,1,0:T(8,128)(2,1)S(1)}, bf16[4,16,4096]{2,1,0:T(8,128)(2,1)S(1)}, u32[]{:S(2)}, u32[]{:S(2)}) collective-permute-start(bf16[4,16,4096]{2,1,0:T(8,128)(2,1)S(1)} %get-tuple-element.9.own_ref), channel_id=1, source_target_pairs={{0,0},{1,1},{2,2},{3,3},{4,4},{5,5},{6,6},{7,7},{9,8},{10,9},{11,1... | collective-permute-start | bytes 1572872 | tf_op jit(solution)/shard_map/ppermute | solution.py:463
  21.8 3.4 %copy-start.10 = (bf16[1,1,1024,4096]{3,2,1,0:T(8,128)(2,1)S(1)}, bf16[1,1,1024,4096]{3,2,1,0:T(8,128)(2,1)}, u32[]{:S(2)}) copy-start(bf16[1,1,1024,4096]{3,2,1,0:T(8,128)(2,1)} %param.16) | copy-start | bytes 25165828
  25.2 0.7 copy-start.11
  25.9 0.7 copy-start.12
  37.0 7.6 %copy-start.1 = (f32[4,16384]{1,0:T(4,128)S(1)}, f32[4,16384]{1,0:T(4,128)}, u32[]{:S(2)}) copy-start(f32[4,16384]{1,0:T(4,128)} %x_ref.3) | copy-start | bytes 786436
  37.0 7.6 %copy-start.3 = (f32[4,16384]{1,0:T(4,128)S(1)}, f32[4,16384]{1,0:T(4,128)}, u32[]{:S(2)}) copy-start(f32[4,16384]{1,0:T(4,128)} %hx_ref.3) | copy-start | bytes 786436
  37.1 7.6 %copy-start.5 = (f32[4,16384]{1,0:T(4,128)S(1)}, f32[4,16384]{1,0:T(4,128)}, u32[]{:S(2)}) copy-start(f32[4,16384]{1,0:T(4,128)} %p_ref.1) | copy-start | bytes 786436
  37.1 7.6 %copy-start.6 = (f32[4,16384]{1,0:T(4,128)S(1)}, f32[4,16384]{1,0:T(4,128)}, u32[]{:S(2)}) copy-start(f32[4,16384]{1,0:T(4,128)} %hp_ref.1) | copy-start | bytes 786436
  37.1 7.5 %collective-permute-start = (bf16[4,16,4096]{2,1,0:T(8,128)(2,1)S(1)}, bf16[4,16,4096]{2,1,0:T(8,128)(2,1)S(1)}, u32[]{:S(2)}, u32[]{:S(2)}) collective-permute-start(bf16[4,16,4096]{2,1,0:T(8,128)(2,1)S(1)} %get-tuple-element.10), channel_id=1, source_target_pairs={{0,0},{1,1},{2,2},{3,3},{4,4},{5,5},{6,6},{7,7},{8,9},{9,10},{10,1... | collective-permute-start | bytes 1572872 | tf_op jit(solution)/shard_map/ppermute | solution.py:465
  85.1 0.7 copy-start.4
  85.8 0.6 copy-start.8

commit v7 on v6

--- a/solution.py
+++ b/solution.py
@@ -16,6 +16,7 @@
 F32 = jnp.float32
 BF16 = jnp.bfloat16
 VMEM_BYTES = 32 * 1024 * 1024
+GATHER_VMEM_BYTES = 58 * 1024 * 1024
 
 
 def row_iota():
@@ -99,7 +100,7 @@
         out_specs=(vmem,) * 2,
         scratch_shapes=[dma((n,)), dma((n,)), dma((n,)), dma((n,))],
         compiler_params=pltpu.CompilerParams(
-            collective_id=0, has_side_effects=True, vmem_limit_bytes=VMEM_BYTES),
+            collective_id=0, has_side_effects=True, vmem_limit_bytes=GATHER_VMEM_BYTES),
     )(x_vec, hx_vec, theta, precond.reshape(1, length))
 
 

time: 88.5 us -> 88.7 us (level)
  local copies, waits for them, and re-layouts: 9.44 us -> 7.11 us
  Pallas kernels: 75.8 us -> 77.4 us
  starting transfers between devices: 1.52 us -> 2.53 us
    pallas_call x1, Pallas kernels: 40.5 us -> 30.6 us  [reduce_pieces(): pl.pallas_call(reduce_kernel, out_shape=(jax.ShapeDtypeStruct(x_vec.shape...]
    pallas_call x1, Pallas kernels: 10.4 us -> 17.4 us  [forward_products(): pl.pallas_call(forward_kernel, out_shape=(jax.ShapeDtypeStruct((slots * s...]
    pallas_call x1, Pallas kernels: 6.69 us -> 9.84 us  [transposed_products(): pl.pallas_call(transposed_kernel, out_shape=jax.ShapeDtypeStruct(far.shap...]
    unnamed x26, local copies, waits for them, and re-layouts: 9.44 us -> 7.11 us
    pallas_call x1, Pallas kernels: 16.4 us -> 17.8 us  [gather_pieces(): pl.pallas_call(gather_kernel, out_shape=(jax.ShapeDtypeStruct((n, GROUPS...]
    ppermute x1, starting transfers between devices: 0.69 us -> 1.7 us  [body(): far = lax.ppermute(own, ('row', 'col'), down)]
  transfers between devices with their start and end apart: 2 -> 2, of which waited for: 0 -> 0; matrix products, arithmetic and copies ran while one was open for 0% -> 0% of each run, Pallas kernels for 19% -> 31%
where the time goes in v7:
time: 88.7 us; the launch traced here: 88.5 us
  Pallas kernels  77.4 us (87%)
  local copies, waits for them, and re-layouts  7.11 us (8%)
  starting transfers between devices  2.53 us (3%)
  between operations  1.47 us (2%)
    pallas_call x1, Pallas kernels, reduce_pieces(): pl.pallas_call(reduce_kernel, out_shape=(jax.ShapeDtypeStruct(x_vec.shape...  30.6 us
    pallas_call x1, Pallas kernels, gather_pieces(): pl.pallas_call(gather_kernel, out_shape=(jax.ShapeDtypeStruct((n, GROUPS...  17.8 us
    pallas_call x1, Pallas kernels, forward_products(): pl.pallas_call(forward_kernel, out_shape=(jax.ShapeDtypeStruct((slots * s...  17.4 us
    pallas_call x1, Pallas kernels, transposed_products(): pl.pallas_call(transposed_kernel, out_shape=jax.ShapeDtypeStruct(far.shap...  9.84 us
    unnamed x26, local copies, waits for them, and re-layouts  7.11 us
  transfers between devices with their start and end apart: 2, of which 0 were waited for; matrix products, arithmetic and copies ran while one was open for 0% of the time, Pallas kernels for 31%

profile of v7, /device:TPU:0, one launch (start us, length us, event | category | flops | bytes accessed | tf_op | source)
XLA Modules:
  0.0 88.5 jit_solution(8443740910915056295)
XLA Ops:
  0.6 0.0 copy-start.12
  0.6 0.0 copy-start.10
  0.7 17.8 %shard_map.121 = (bf16[4,16,4096]{2,1,0:T(8,128)(2,1)}, f32[4,16384]{1,0:T(4,128)}) custom-call(f32[4,16384]{1,0:T(4,128)} %x_ref.3, f32[4,16384]{1,0:T(4,128)} %hx_ref.3, f32[4]{0:T(128)} %theta_ref.1, f32[1,16384]{1,0:T(1,128)} %bitcast.12), custom_call_target="tpu_custom_call" | custom-call | tf_op jit(solution)/shard_map/pallas_call | solution.py:93
  18.5 1.7 %collective-permute-start.1 = (bf16[4,16,4096]{2,1,0:T(8,128)(2,1)}, bf16[4,16,4096]{2,1,0:T(8,128)(2,1)S(1)}, u32[]{:S(2)}, u32[]{:S(2)}) collective-permute-start(bf16[4,16,4096]{2,1,0:T(8,128)(2,1)} %get-tuple-element.9.own_ref), channel_id=1, source_target_pairs={{0,0},{1,1},{2,2},{3,3},{4,4},{5,5},{6,6},{7,7},{9,8},{10,9},{11,1... | collective-permute-start | bytes 1572872 | tf_op jit(solution)/shard_map/ppermute | solution.py:464
  20.8 0.0 copy-start.7
  20.9 3.4 %copy-done.7 = bf16[1,1,1024,4096]{3,2,1,0:T(8,128)(2,1)S(1)} copy-done((bf16[1,1,1024,4096]{3,2,1,0:T(8,128)(2,1)S(1)}, bf16[1,1,1024,4096]{3,2,1,0:T(8,128)(2,1)}, u32[]{:S(2)}) %copy-start.7) | copy-done | bytes 8388632
  24.2 0.0 copy-start.8
  24.2 1.0 %copy-done.8 = bf16[4,16,4096]{2,1,0:T(8,128)(2,1)S(1)} copy-done((bf16[4,16,4096]{2,1,0:T(8,128)(2,1)S(1)}, bf16[4,16,4096]{2,1,0:T(8,128)(2,1)}, u32[]{:S(2)}) %copy-start.8) | copy-done | bytes 524312
  25.3 0.0 copy-start.9
  25.3 0.7 copy-done.9
  26.0 0.0 copy-start.11
  26.0 0.7 copy-done.11
  26.6 17.4 %shard_map.122 = (bf16[32768,128]{1,0:T(8,128)(2,1)S(1)}, bf16[4,16,4096]{2,1,0:T(8,128)(2,1)S(1)}) custom-call(s32[1024]{0:T(1024)S(1)} %bitcast.8, s32[1024]{0:T(1024)S(1)} %bitcast.10, s32[1]{0:T(128)} %bitcast.5.count_ref, bf16[1024,4096]{1,0:T(8,128)(2,1)S(1)} %bitcast.7, bf16[4,16,4096]{2,1,0:T(8,128)(2,1)S(1)} %copy-done.8), custom_call_target="tpu_custom_call" | custom-call | flops 4294967296 | bytes 16777216 | tf_op jit(solution)/shard_map/pallas_call | solution.py:272
  44.0 0.0 copy-start
  44.0 0.0 copy-start.1
  44.0 0.0 copy-start.3
  44.0 0.0 copy-start.4
  44.1 0.0 copy-start.5
  44.1 0.8 collective-permute-start
  44.9 0.0 collective-permute-done.1.far_ref
  44.9 0.0 copy-done.12
  44.9 0.0 copy-done.10
  44.9 9.8 %shard_map.123.tr_ref = f32[4,16,4096]{2,1,0:T(8,128)S(1)} custom-call(s32[1024]{0:T(1024)S(1)} %bitcast.9, s32[1024]{0:T(1024)S(1)} %bitcast.11, s32[1]{0:T(128)} %bitcast.6.count_ref, bf16[32768,128]{1,0:T(8,128)(2,1)S(1)} %get-tuple-element.11.packed, bf16[4,16,4096]{2,1,0:T(8,128)(2,1)S(1)} %collective-permute-done.1.far_ref), custom_call_target="tpu_custom_call" | custom-call | flops 4294967296 | bytes 16777216 | tf_op jit(solution)/shard_map/pallas_call | solution.py:297
  54.8 0.0 collective-permute-done.came_ref
  54.8 0.0 copy-done
  54.8 0.0 copy-done.1
  54.8 0.0 copy-done.3
  54.8 0.0 copy-done.4
  54.8 0.0 copy-done.5
  54.8 30.6 %shard_map.124 = (f32[4,16384]{1,0:T(4,128)S(1)}, f32[24,128]{1,0:T(8,128)S(1)}) custom-call(bf16[4,16,4096]{2,1,0:T(8,128)(2,1)S(1)} %collective-permute-done.came_ref, f32[4,16,4096]{2,1,0:T(8,128)S(1)} %shard_map.123.tr_ref, f32[4,16384]{1,0:T(4,128)S(1)} %copy-done, f32[4,16384]{1,0:T(4,128)S(1)} %copy-done.5, f32[4,16384]{1,0:T(4,128)S(1)} %copy-done.3, ...), custom_call_target="tpu_custom_call" | custom-call | tf_op jit(solution)/shard_map/pallas_call | solution.py:412
  85.5 0.0 copy-start.2
  85.5 0.7 copy-done.2
  86.1 0.0 copy-start.6
  86.1 0.6 copy-done.6
  86.7 1.7 %shard_map.125 = (f32[4,16384]{1,0:T(4,128)}, f32[12,12]{1,0:T(8,128)}, f32[12,12]{1,0:T(8,128)}) custom-call(f32[4,16384]{1,0:T(4,128)} %copy-done.2, f32[24,128]{1,0:T(8,128)} %copy-done.6), custom_call_target="tpu_custom_call" | custom-call | tf_op jit(solution)/shard_map/pallas_call | solution.py:448
Async XLA Ops:
  0.6 44.3 %copy-start.12 = (s32[1,1,1024]{2,1,0:T(1,128)S(1)}, s32[1,1,1024]{2,1,0:T(1,128)}, u32[]{:S(2)}) copy-start(s32[1,1,1024]{2,1,0:T(1,128)} %param.18) | copy-start | bytes 12292
  0.6 44.3 %copy-start.10 = (s32[1,1,1024]{2,1,0:T(1,128)S(1)}, s32[1,1,1024]{2,1,0:T(1,128)}, u32[]{:S(2)}) copy-start(s32[1,1,1024]{2,1,0:T(1,128)} %param.17) | copy-start | bytes 12292
  18.5 26.4 %collective-permute-start.1 = (bf16[4,16,4096]{2,1,0:T(8,128)(2,1)}, bf16[4,16,4096]{2,1,0:T(8,128)(2,1)S(1)}, u32[]{:S(2)}, u32[]{:S(2)}) collective-permute-start(bf16[4,16,4096]{2,1,0:T(8,128)(2,1)} %get-tuple-element.9.own_ref), channel_id=1, source_target_pairs={{0,0},{1,1},{2,2},{3,3},{4,4},{5,5},{6,6},{7,7},{9,8},{10,9},{11,1... | collective-permute-start | bytes 1572872 | tf_op jit(solution)/shard_map/ppermute | solution.py:464
  20.8 3.4 %copy-start.7 = (bf16[1,1,1024,4096]{3,2,1,0:T(8,128)(2,1)S(1)}, bf16[1,1,1024,4096]{3,2,1,0:T(8,128)(2,1)}, u32[]{:S(2)}) copy-start(bf16[1,1,1024,4096]{3,2,1,0:T(8,128)(2,1)} %param.16) | copy-start | bytes 25165828
  24.2 1.0 %copy-start.8 = (bf16[4,16,4096]{2,1,0:T(8,128)(2,1)S(1)}, bf16[4,16,4096]{2,1,0:T(8,128)(2,1)}, u32[]{:S(2)}) copy-start(bf16[4,16,4096]{2,1,0:T(8,128)(2,1)} %get-tuple-element.9.own_ref) | copy-start | bytes 1572868
  25.3 0.7 copy-start.9
  26.0 0.7 copy-start.11
  44.0 10.8 %copy-start = (f32[4,16384]{1,0:T(4,128)S(1)}, f32[4,16384]{1,0:T(4,128)}, u32[]{:S(2)}) copy-start(f32[4,16384]{1,0:T(4,128)} %x_ref.3) | copy-start | bytes 786436
  44.0 10.8 %copy-start.1 = (f32[4,16384]{1,0:T(4,128)S(1)}, f32[4,16384]{1,0:T(4,128)}, u32[]{:S(2)}) copy-start(f32[4,16384]{1,0:T(4,128)} %hx_ref.3) | copy-start | bytes 786436
  44.0 10.8 %copy-start.3 = (f32[4,16384]{1,0:T(4,128)S(1)}, f32[4,16384]{1,0:T(4,128)}, u32[]{:S(2)}) copy-start(f32[4,16384]{1,0:T(4,128)} %p_ref.1) | copy-start | bytes 786436
  44.0 10.8 %copy-start.4 = (f32[4,16384]{1,0:T(4,128)S(1)}, f32[4,16384]{1,0:T(4,128)}, u32[]{:S(2)}) copy-start(f32[4,16384]{1,0:T(4,128)} %hp_ref.1) | copy-start | bytes 786436
  44.1 10.8 %copy-start.5 = (f32[4,16384]{1,0:T(4,128)S(1)}, f32[4,16384]{1,0:T(4,128)}, u32[]{:S(2)}) copy-start(f32[4,16384]{1,0:T(4,128)} %get-tuple-element.12.res_ref) | copy-start | bytes 786436
  44.1 10.7 %collective-permute-start = (bf16[4,16,4096]{2,1,0:T(8,128)(2,1)S(1)}, bf16[4,16,4096]{2,1,0:T(8,128)(2,1)S(1)}, u32[]{:S(2)}, u32[]{:S(2)}) collective-permute-start(bf16[4,16,4096]{2,1,0:T(8,128)(2,1)S(1)} %get-tuple-element.10), channel_id=1, source_target_pairs={{0,0},{1,1},{2,2},{3,3},{4,4},{5,5},{6,6},{7,7},{8,9},{9,10},{10,1... | collective-permute-start | bytes 1572872 | tf_op jit(solution)/shard_map/ppermute | solution.py:466
  85.5 0.7 copy-start.2
  86.1 0.6 copy-start.6
